TPU v7x, 128 devices: a whole 4x4x4 slice. The times are simulated.
128 devices in a mesh: dp: 8 (over x, core), seq: 16 (over y, z).
Axes of the slice: x: 4, y: 4, z: 4, core: 2. Of those that a mesh axis runs over, the one named last changes fastest.
Arguments:
- hidden: bfloat16 [16384, 8192], P(('dp', 'seq')), may hold values from -24 to 24
- queries: bfloat16 [16384, 4096], P(('dp', 'seq')), may hold values from -120 to 120
- kv_weight: bfloat16 [8192, 1024], replicated, may hold values from -0.0625 to 0.0625
- value_projection_bias: float32 [512], replicated, may hold values from -4 to 4
- cotangent: bfloat16 [16384, 4096], P(('dp', 'seq')), may hold values from -6 to 6
- lengths: int32 [8, 8], P('dp'), may hold values from 1 to 1024, 2048 in all within a row
Outputs:
- attended: bfloat16 [16384, 4096], P(('dp', 'seq'))
- query_grad: bfloat16 [16384, 4096], P(('dp', 'seq'))
- hidden_grad: bfloat16 [16384, 8192], P(('dp', 'seq'))
- weight_grad: float32 [8192, 1024], P(('dp', 'seq'))
Inputs may be any that keep to these rules, and one draw needn't show every extreme that they name: The lengths of a row sum to 2048; in every row the longest document has exactly 1024 tokens.
All inputs are finite; a program needn't handle non-finite values.
Results may differ from a plain program's by a relative error of at most 0.025.
Values may be sent and summed in bfloat16 or wider, within the bound.
A program may use at most 192 MiB of HBM per device.

v0:
```python
import math

import jax
import jax.numpy as jnp
from jax import lax
from jax.sharding import PartitionSpec as P

QUERY_HEADS = 32
KEY_VALUE_HEADS = 4
HEAD_SIZE = 128


def attend(query_heads, key_value_pair, grad_heads, doc_ids):
    row_width_total = query_heads.shape[0]
    head_count = query_heads.shape[1]
    block_rows = min(512, row_width_total)
    block_count = row_width_total // block_rows
    score_scale = 1.0 / math.sqrt(HEAD_SIZE)
    key_part = key_value_pair[:, :HEAD_SIZE]
    value_part = key_value_pair[:, HEAD_SIZE:]
    position = jnp.arange(row_width_total, dtype=jnp.int32)

    def block_step(running, sliced):
        query_block, grad_block, doc_block, pos_block = sliced
        scores = (
            jnp.einsum("qhd,kd->hqk", query_block, key_part, preferred_element_type=jnp.float32)
            * score_scale
        )
        allowed = (doc_block[:, None] == doc_ids[None, :]) & (
            position[None, :] <= pos_block[:, None]
        )
        scores = jnp.where(allowed[None], scores, -1e30)
        row_max = jnp.max(scores, axis=-1, keepdims=True)
        weights_raw = jnp.where(allowed[None], jnp.exp(scores - row_max), 0.0)
        probability = weights_raw / jnp.sum(weights_raw, axis=-1, keepdims=True)
        prob_half = probability.astype(jnp.bfloat16)
        out_block = jnp.einsum(
            "hqk,kd->qhd", prob_half, value_part, preferred_element_type=jnp.float32
        ).astype(jnp.bfloat16)
        row_delta = jnp.sum(grad_block.astype(jnp.float32) * out_block.astype(jnp.float32), axis=-1)
        prob_grad = jnp.einsum(
            "qhd,kd->hqk", grad_block, value_part, preferred_element_type=jnp.float32
        )
        score_grad = (probability * (prob_grad - row_delta.T[:, :, None]) * score_scale).astype(
            jnp.bfloat16
        )
        query_grad = jnp.einsum(
            "hqk,kd->qhd", score_grad, key_part, preferred_element_type=jnp.float32
        ).astype(jnp.bfloat16)
        key_grad = running[0] + jnp.einsum(
            "hqk,qhd->kd", score_grad, query_block, preferred_element_type=jnp.float32
        )
        value_grad = running[1] + jnp.einsum(
            "hqk,qhd->kd", prob_half, grad_block, preferred_element_type=jnp.float32
        )
        return ((key_grad, value_grad), (out_block, query_grad))

    sliced = (
        query_heads.reshape(block_count, block_rows, head_count, HEAD_SIZE),
        grad_heads.reshape(block_count, block_rows, head_count, HEAD_SIZE),
        doc_ids.reshape(block_count, block_rows),
        position.reshape(block_count, block_rows),
    )
    zero_grads = (
        jnp.zeros((row_width_total, HEAD_SIZE), jnp.float32),
        jnp.zeros((row_width_total, HEAD_SIZE), jnp.float32),
    )
    (key_grad, value_grad), (out_blocks, grad_blocks) = lax.scan(block_step, zero_grads, sliced)
    return (
        out_blocks.reshape(row_width_total, head_count, HEAD_SIZE),
        grad_blocks.reshape(row_width_total, head_count, HEAD_SIZE),
        jnp.concatenate([key_grad, value_grad], axis=1),
    )


def local(hidden, queries, kv_weight, value_projection_bias, cotangent, lengths):
    token_count = hidden.shape[0]
    sequence_count = lax.axis_size("seq")
    data_count = lax.axis_size("dp")
    row_width_total = token_count * sequence_count
    key_value_columns = 2 * KEY_VALUE_HEADS * HEAD_SIZE
    repeat_count = sequence_count // KEY_VALUE_HEADS
    factor = 1.0 / math.sqrt(row_width_total * data_count)
    query_heads = queries.reshape(token_count, QUERY_HEADS, HEAD_SIZE)
    grad_heads = cotangent.reshape(token_count, QUERY_HEADS, HEAD_SIZE)
    query_local, grad_local = (
        lax.all_to_all(query_heads, "seq", split_axis=1, concat_axis=0, tiled=True),
        lax.all_to_all(grad_heads, "seq", split_axis=1, concat_axis=0, tiled=True),
    )
    complete_bias = jnp.stack(
        [
            jnp.zeros((KEY_VALUE_HEADS, HEAD_SIZE), jnp.float32),
            value_projection_bias.reshape(KEY_VALUE_HEADS, HEAD_SIZE),
        ],
        axis=1,
    ).reshape(key_value_columns)
    key_value_pair = (
        jnp.dot(hidden, kv_weight, preferred_element_type=jnp.float32) + complete_bias
    ).astype(jnp.bfloat16)
    expanded = jnp.broadcast_to(
        key_value_pair.reshape(token_count, KEY_VALUE_HEADS, 1, 2 * HEAD_SIZE),
        (token_count, KEY_VALUE_HEADS, repeat_count, 2 * HEAD_SIZE),
    )
    expanded = expanded.reshape(token_count, sequence_count, 2 * HEAD_SIZE)
    kv_local = lax.all_to_all(expanded, "seq", split_axis=1, concat_axis=0, tiled=True).reshape(
        row_width_total, 2 * HEAD_SIZE
    )
    position = jnp.arange(row_width_total, dtype=jnp.int32)
    doc_ends = jnp.cumsum(lengths[0])
    doc_ids = jnp.sum((position[:, None] >= doc_ends[None, :]).astype(jnp.int32), axis=1)
    out_heads, qgrad_heads, kv_grad_local = attend(query_local, kv_local, grad_local, doc_ids)
    attended, query_grad = (
        lax.all_to_all(out_heads, "seq", split_axis=0, concat_axis=1, tiled=True),
        lax.all_to_all(qgrad_heads, "seq", split_axis=0, concat_axis=1, tiled=True),
    )
    key_value_pieces = lax.all_to_all(
        kv_grad_local.reshape(row_width_total, 1, 2 * HEAD_SIZE),
        "seq",
        split_axis=0,
        concat_axis=1,
        tiled=True,
    )
    key_value_gradient = jnp.sum(
        key_value_pieces.reshape(token_count, KEY_VALUE_HEADS, repeat_count, 2 * HEAD_SIZE), axis=2
    ).reshape(token_count, key_value_columns)
    key_value_gradient = key_value_gradient.astype(jnp.bfloat16)
    hidden_grad = jnp.einsum(
        "tc,dc->td", key_value_gradient, kv_weight, preferred_element_type=jnp.float32
    ).astype(jnp.bfloat16)
    product = lax.dot_general(
        hidden, key_value_gradient, (((0,), (0,)), ((), ())), preferred_element_type=jnp.float32
    )
    weight_grad = lax.psum_scatter(product * factor, ("dp", "seq"), scatter_dimension=0, tiled=True)
    return (
        attended.reshape(token_count, QUERY_HEADS * HEAD_SIZE),
        query_grad.reshape(token_count, QUERY_HEADS * HEAD_SIZE),
        hidden_grad,
        weight_grad,
    )


def solution(mesh):
    in_specs = (
        P(("dp", "seq"), None),
        P(("dp", "seq"), None),
        P(),
        P(),
        P(("dp", "seq"), None),
        P("dp", None),
    )
    out_specs = (
        P(("dp", "seq"), None),
        P(("dp", "seq"), None),
        P(("dp", "seq"), None),
        P(("dp", "seq"), None),
    )
    return jax.shard_map(local, mesh=mesh, in_specs=in_specs, out_specs=out_specs, check_vma=False)
```

profile of v0, /device:TPU:0, one launch (start us, length us, event | category | flops | bytes accessed | tf_op | source)
XLA Modules:
  0.0 1003.6 jit_solution(15269479508968949172)
XLA Ops:
  8.8 8.1 fusion.55
  18.2 8.1 all-to-all-start.1
  28.7 15.4 %all-to-all-done.1 = bf16[128,16,256]{0,2,1:T(8,128)(2,1)S(1)} async-done(((bf16[128,16,256]{0,2,1:T(8,128)(2,1)}), bf16[128,16,256]{0,2,1:T(8,128)(2,1)S(1)}, u32[]{:S(2)}, u32[]{:S(2)}) %all-to-all-start.1) | async-done | bytes 1048608 | tf_op jit(solution)/shard_map/all_to_all | solution.py:105
  44.1 4.3 all-to-all-start.2
  50.7 12.8 %all-to-all-done.2 = bf16[128,32,128]{0,2,1:T(8,128)(2,1)} async-done(((bf16[128,32,128]{0,2,1:T(8,128)(2,1)}), bf16[128,32,128]{0,2,1:T(8,128)(2,1)}, u32[]{:S(2)}, u32[]{:S(2)}) %all-to-all-start.2) | async-done | bytes 1048608 | tf_op jit(solution)/shard_map/all_to_all | solution.py:88
  77.1 5.4 all-to-all-done
  84.7 131.7 %while.17 = (s32[]{:T(128)}, f32[2048,128]{1,0:T(8,128)S(1)}, f32[2048,128]{1,0:T(8,128)}, bf16[4,512,2,128]{3,1,0,2:T(8,128)(2,1)}, bf16[4,512,2,128]{3,1,0,2:T...) while((s32[]{:T(128)}, f32[2048,128]{1,0:T(8,128)S(1)}, ...), condition=%wide.region_6.7_spmd.clone, body=%wide.region_2.6_spmd.clone.sunk | while | flops 3251373056 | bytes 146058112 | solution.py:68
  87.0 9.1 fusion.106
  96.2 4.8 fusion.107
  119.6 9.2 fusion.106
  128.8 4.8 fusion.107
  152.7 9.2 fusion.106
  161.9 4.8 fusion.107
  185.7 9.2 fusion.106
  194.9 4.8 fusion.107
  219.3 29.9 %all_to_all.90 = f32[2048,1,256]{2,1,0:T(1,128)S(1)} all-to-all(f32[2048,1,256]{2,1,0:T(1,128)S(1)} %reshape.169), channel_id=1, replica_groups=mesh['dp'=8,'seq'=16] {'seq'}, dimensions={0} | all-to-all | bytes 4194304 | tf_op jit(solution)/shard_map/all_to_all | solution.py:116
  249.7 13.1 %multiply_bitcast_fusion = f32[8192,1024]{0,1:T(8,128)} fusion(bf16[128,1024]{0,1:T(8,128)(2,1)S(1)} %bitcast.203, bf16[128,8192]{1,0:T(8,128)(2,1)S(1)} %copy-done), kind=kOutput, calls=%fused_computation.55 | convolution fusion | flops 2155872256 | bytes 35913728 | tf_op jit(solution)/shard_map/dot_general | solution.py:130
  262.8 33.4 %copy.153 = f32[8192,1024]{1,0:T(8,128)} copy(f32[8192,1024]{0,1:T(8,128)} %multiply_bitcast_fusion) | data formatting | bytes 67108864
  297.4 9.4 copy.134
  314.1 15.5 %all-to-all-done.3 = bf16[2048,2,128]{2,1,0:T(2,128)(2,1)S(1)} async-done(((bf16[2048,2,128]{2,1,0:T(2,128)(2,1)}), bf16[2048,2,128]{2,1,0:T(2,128)(2,1)S(1)}, u32[]{:S(2)}, u32[]{:S(2)}) %all-to-all-start.3) | async-done | bytes 1048608 | tf_op jit(solution)/shard_map/all_to_all | solution.py:113
  329.6 6.4 all-to-all-start.4
  340.1 16.5 %all-to-all-done.4 = bf16[2048,2,128]{2,1,0:T(2,128)(2,1)} async-done(((bf16[2048,2,128]{2,1,0:T(2,128)(2,1)}), bf16[2048,2,128]{2,1,0:T(2,128)(2,1)}, u32[]{:S(2)}, u32[]{:S(2)}) %all-to-all-start.4) | async-done | bytes 1048608 | tf_op jit(solution)/shard_map/all_to_all | solution.py:114
  361.5 12.9 %convolution_convert_fusion.2 = bf16[128,8192]{1,0:T(8,128)(2,1)} fusion(bf16[128,1024]{0,1:T(8,128)(2,1)S(1)} %bitcast.204, bf16[8192,1024]{1,0:T(8,128)(2,1)} %param.10), kind=kOutput, calls=%fused_computation.56 | convolution fusion | flops 2148532224 | bytes 19136512 | tf_op jit(solution)/shard_map/tc,dc->td/dot_general | solution.py:127
  374.4 622.4 %reduce-scatter.4.cloned.1.call-done = f32[64,1024]{1,0:T(8,128)} async-done(((f32[8192,1024]{1,0:T(8,128)}), f32[64,1024]{1,0:T(8,128)}) %reduce-scatter.4.cloned.1.call-update) | async-done | bytes 262160
  (142 shorter events, 119.6 us)
Async XLA Ops:
  18.2 25.8 %all-to-all-start.1 = ((bf16[128,16,256]{0,2,1:T(8,128)(2,1)}), bf16[128,16,256]{0,2,1:T(8,128)(2,1)S(1)}, u32[]{:S(2)}, u32[]{:S(2)}) async-start(bf16[128,16,256]{0,2,1:T(8,128)(2,1)} %bitcast.10), calls=%async_computation.1 | async-start | bytes 2097152 | tf_op jit(solution)/shard_map/all_to_all | solution.py:105
  26.4 41.6 %copy-start.9 = (s32[1,8]{1,0:T(1,128)S(1)}, s32[1,8]{1,0:T(1,128)}, u32[]{:S(2)}) copy-start(s32[1,8]{1,0:T(1,128)} %param.13) | copy-start | bytes 100
  44.1 23.8 %copy-start.5 = (bf16[128,16,256]{0,2,1:T(8,128)(2,1)}, bf16[128,16,256]{0,2,1:T(8,128)(2,1)S(1)}, u32[]{:S(2)}) copy-start(bf16[128,16,256]{0,2,1:T(8,128)(2,1)S(1)} %all-to-all-done.1) | copy-start | bytes 3145732
  44.1 19.4 %all-to-all-start.2 = ((bf16[128,32,128]{0,2,1:T(8,128)(2,1)}), bf16[128,32,128]{0,2,1:T(8,128)(2,1)}, u32[]{:S(2)}, u32[]{:S(2)}) async-start(bf16[128,32,128]{0,2,1:T(8,128)(2,1)} %bitcast.197), calls=%async_computation.2 | async-start | bytes 2097152 | tf_op jit(solution)/shard_map/all_to_all | solution.py:88
  63.5 19.0 %all-to-all-start = ((bf16[128,32,128]{0,2,1:T(8,128)(2,1)}), bf16[128,32,128]{0,2,1:T(8,128)(2,1)}, u32[]{:S(2)}, u32[]{:S(2)}) async-start(bf16[128,32,128]{0,2,1:T(8,128)(2,1)} %bitcast.196), calls=%async_computation | async-start | bytes 2097152 | tf_op jit(solution)/shard_map/all_to_all | solution.py:87
  67.9 928.9 %reduce-scatter.4.cloned.1.call-start = ((), (), s32[]{:S(2)}) async-start(), calls=%async_computation.7 | async-start | bytes 33816576
  96.1 8.2 slice-start
  96.1 6.8 copy-start.4
  96.1 6.8 copy-start.7
  96.2 8.1 slice-start.1
  128.8 8.1 slice-start
  128.8 6.8 copy-start.4
  128.8 6.8 copy-start.7
  128.8 8.1 slice-start.1
  161.8 8.1 slice-start
  161.8 6.8 copy-start.4
  161.8 6.8 copy-start.7
  161.9 8.1 slice-start.1
  194.9 8.1 slice-start
  194.9 6.8 copy-start.4
  194.9 6.8 copy-start.7
  194.9 8.1 slice-start.1
  306.9 22.8 %all-to-all-start.3 = ((bf16[2048,2,128]{2,1,0:T(2,128)(2,1)}), bf16[2048,2,128]{2,1,0:T(2,128)(2,1)S(1)}, u32[]{:S(2)}, u32[]{:S(2)}) async-start(bf16[2048,2,128]{2,1,0:T(2,128)(2,1)} %copy.134), calls=%async_computation.3 | async-start | bytes 2097152 | tf_op jit(solution)/shard_map/all_to_all | solution.py:113
  329.6 26.9 %all-to-all-start.4 = ((bf16[2048,2,128]{2,1,0:T(2,128)(2,1)}), bf16[2048,2,128]{2,1,0:T(2,128)(2,1)}, u32[]{:S(2)}, u32[]{:S(2)}) async-start(bf16[2048,2,128]{2,1,0:T(2,128)(2,1)} %copy.138), calls=%async_computation.4 | async-start | bytes 2097152 | tf_op jit(solution)/shard_map/all_to_all | solution.py:114
  (18 other events, 52.8 us)
Sparse Core Ops, SparseCore 0:
  296.4 700.3 reduce-scatter.3
where the time goes:
time: 1010 us; the launch traced here: 1000 us
  waiting for transfers between devices  688 us (68%)
  matrix products  126 us (12%)
  local copies, waits for them, and re-layouts  88 us (9%)
  other arithmetic  30 us (3%)
  blocking collectives  29.9 us (3%)
  starting transfers between devices  26.9 us (3%)
  between operations  14.2 us (1%)
    unnamed x2, waiting for transfers between devices  622 us
    unnamed x15, local copies, waits for them, and re-layouts  45.7 us
    sub x4, matrix products, block_step(): weights_raw = jnp.where(allowed[None], jnp.exp(scores - row_max), 0.0)  36.7 us
    all_to_all x1, blocking collectives, local(): lax.all_to_all(kv_grad_local.reshape(row_width_total, 1, 2 * HEAD_SIZE),...  29.9 us
  transfers between devices with their start and end apart: 6, of which 6 were waited for; matrix products, arithmetic and copies ran while one was open for 5% of the time, Pallas kernels for 0%

commit v1 on v0

--- a/solution.py
+++ b/solution.py
@@ -127,10 +127,17 @@
     hidden_grad = jnp.einsum(
         "tc,dc->td", key_value_gradient, kv_weight, preferred_element_type=jnp.float32
     ).astype(jnp.bfloat16)
+    hidden_columns = lax.all_to_all(
+        hidden.reshape(token_count, data_count, -1), "dp", split_axis=1, concat_axis=0, tiled=True
+    ).reshape(token_count * data_count, -1)
+    gathered_gradient = lax.all_gather(key_value_gradient, "dp", axis=0, tiled=True)
     product = lax.dot_general(
-        hidden, key_value_gradient, (((0,), (0,)), ((), ())), preferred_element_type=jnp.float32
+        hidden_columns,
+        gathered_gradient,
+        (((0,), (0,)), ((), ())),
+        preferred_element_type=jnp.float32,
     )
-    weight_grad = lax.psum_scatter(product * factor, ("dp", "seq"), scatter_dimension=0, tiled=True)
+    weight_grad = lax.psum_scatter(product * factor, "seq", scatter_dimension=0, tiled=True)
     return (
         attended.reshape(token_count, QUERY_HEADS * HEAD_SIZE),
         query_grad.reshape(token_count, QUERY_HEADS * HEAD_SIZE),

time: 1010 us -> 377 us (0.37)
  the two profiles are of different devices: /device:TPU:0 before, /device:TPU:1 now
where the time goes in v1:
time: 377 us; the launch traced here: 371 us
  matrix products  98.9 us (26%)
  waiting for transfers between devices  77.2 us (20%)
  blocking collectives  73.6 us (20%)
  local copies, waits for them, and re-layouts  55.3 us (15%)
  starting transfers between devices  25.9 us (7%)
  other arithmetic  24.4 us (6%)
  between operations  14.5 us (4%)
    all_to_all x1, blocking collectives, local(): lax.all_to_all(hidden.reshape(token_count, data_count, -1), 'dp', split_a...  42.4 us
    sub x4, matrix products, block_step(): weights_raw = jnp.where(allowed[None], jnp.exp(scores - row_max), 0.0)  33.9 us
    all_to_all x1, blocking collectives, local(): lax.all_to_all(kv_grad_local.reshape(row_width_total, 1, 2 * HEAD_SIZE),...  31.2 us
    convert_element_type x4, other arithmetic, block_step(): prob_half = probability.astype(jnp.bfloat16)  19.1 us
    unnamed x3, waiting for transfers between devices  17 us
    unnamed x22, local copies, waits for them, and re-layouts  16.9 us
    all_to_all x1, waiting for transfers between devices, local(): lax.all_to_all(out_heads, 'seq', split_axis=0, concat_axis=1, tiled=True)  16.6 us
    all_to_all x1, waiting for transfers between devices, local(): lax.all_to_all(expanded, 'seq', split_axis=1, concat_axis=0, tiled=True)  14.2 us
  transfers between devices with their start and end apart: 7, of which 6 were waited for; matrix products, arithmetic and copies ran while one was open for 14% of the time, Pallas kernels for 0%

profile of v1, /device:TPU:1, one launch (start us, length us, event | category | flops | bytes accessed | tf_op | source)
XLA Modules:
  0.0 370.9 jit_solution(18360057654624701144)
XLA Ops:
  7.9 8.7 %fusion.55 = bf16[128,1024]{1,0:T(8,128)(2,1)S(1)} fusion(bf16[128,8192]{1,0:T(8,128)(2,1)} %param.8, bf16[8192,1024]{1,0:T(8,128)(2,1)} %param.10, f32[1024]{0:T(1024)S(1)} %bitcast.217), kind=kOutput, calls=%fused_computation.60 | convolution fusion | flops 2147745792 | bytes 19140608 | tf_op jit(solution)/shard_map/dot_general | solution.py:98
  18.0 8.6 %all-to-all-start.1 = ((bf16[128,16,256]{0,2,1:T(8,128)(2,1)}), bf16[128,16,256]{0,2,1:T(8,128)(2,1)S(1)}, u32[]{:S(2)}, u32[]{:S(2)}) async-start(bf16[128,16,256]{0,2,1:T(8,128)(2,1)} %bitcast.10), calls=%async_computation.1 | async-start | bytes 2097152 | tf_op jit(solution)/shard_map/all_to_all | solution.py:105
  27.9 14.2 %all-to-all-done.1 = bf16[128,16,256]{0,2,1:T(8,128)(2,1)S(1)} async-done(((bf16[128,16,256]{0,2,1:T(8,128)(2,1)}), bf16[128,16,256]{0,2,1:T(8,128)(2,1)S(1)}, u32[]{:S(2)}, u32[]{:S(2)}) %all-to-all-start.1) | async-done | bytes 1048608 | tf_op jit(solution)/shard_map/all_to_all | solution.py:105
  48.3 12.1 %all-to-all-done = bf16[128,32,128]{0,2,1:T(8,128)(2,1)S(1)} async-done(((bf16[128,32,128]{0,2,1:T(8,128)(2,1)}), bf16[128,32,128]{0,2,1:T(8,128)(2,1)S(1)}, u32[]{:S(2)}, u32[]{:S(2)}) %all-to-all-start) | async-done | bytes 1048608 | tf_op jit(solution)/shard_map/all_to_all | solution.py:87
  60.4 5.3 %all-to-all-start.2 = ((bf16[128,32,128]{0,2,1:T(8,128)(2,1)}), bf16[128,32,128]{0,2,1:T(8,128)(2,1)}, u32[]{:S(2)}, u32[]{:S(2)}) async-start(bf16[128,32,128]{0,2,1:T(8,128)(2,1)} %bitcast.14), calls=%async_computation.2 | async-start | bytes 2097152 | tf_op jit(solution)/shard_map/all_to_all | solution.py:88
  72.8 7.3 %all-to-all-done.2 = bf16[128,32,128]{0,2,1:T(8,128)(2,1)} async-done(((bf16[128,32,128]{0,2,1:T(8,128)(2,1)}), bf16[128,32,128]{0,2,1:T(8,128)(2,1)}, u32[]{:S(2)}, u32[]{:S(2)}) %all-to-all-start.2) | async-done | bytes 1048608 | tf_op jit(solution)/shard_map/all_to_all | solution.py:88
  82.4 98.8 %while.17 = (s32[]{:T(128)}, f32[2048,128]{1,0:T(8,128)S(1)}, f32[2048,128]{1,0:T(8,128)S(1)}, bf16[4,512,2,128]{3,1,0,2:T(8,128)(2,1)}, bf16[4,512,2,128]{3,1,0...) while((s32[]{:T(128)}, f32[2048,128]{1,0:T(8,128)S(1)}, ...), condition=%wide.region_6.7_spmd.clone, body=%wide.region_2.6_spmd.clone.sunk | while | flops 3251373056 | bytes 95723848 | solution.py:68
  84.0 8.5 %fusion.106 = (f32[2,512]{1,0:T(2,128)S(1)}, f32[2,512,2048]{2,1,0:T(8,128)}) fusion(pred[512,2048]{1,0:T(8,128)(4,1)S(1)} %fusion.105, bf16[2048,128]{1,0:T(8,128)(2,1)} %get-tuple-element.385, bf16[4,512,2,128]{3,1,0,2:T(8,128)(2,1)} %get-tuple-element.384, s32[]{:T(128)S(6)} %copy.179), kind=kOutput, calls=%fused_computation.64.clone.1 | convolution fusion | flops 547358720 | bytes 11276292 | tf_op jit(solution)/shard_map/while/body/eval_jaxpr/sub | solution.py:34
  92.5 4.8 %fusion.107 = bf16[2,512,2048]{2,1,0:T(8,128)(2,1)S(1)} fusion(f32[2,512,2048]{2,1,0:T(8,128)} %get-tuple-element.344, f32[2,512]{1,0:T(2,128)S(1)} %get-tuple-element.345), kind=kLoop, calls=%fused_computation.18.clone.1 | loop fusion | flops 4194304 | bytes 12587008 | tf_op jit(solution)/shard_map/while/body/eval_jaxpr/convert_element_type | solution.py:36
  108.6 8.5 %fusion.106 = (f32[2,512]{1,0:T(2,128)S(1)}, f32[2,512,2048]{2,1,0:T(8,128)}) fusion(pred[512,2048]{1,0:T(8,128)(4,1)S(1)} %fusion.105, bf16[2048,128]{1,0:T(8,128)(2,1)} %get-tuple-element.385, bf16[4,512,2,128]{3,1,0,2:T(8,128)(2,1)} %get-tuple-element.384, s32[]{:T(128)S(6)} %copy.179), kind=kOutput, calls=%fused_computation.64.clone.1 | convolution fusion | flops 547358720 | bytes 11276292 | tf_op jit(solution)/shard_map/while/body/eval_jaxpr/sub | solution.py:34
  117.1 4.8 %fusion.107 = bf16[2,512,2048]{2,1,0:T(8,128)(2,1)S(1)} fusion(f32[2,512,2048]{2,1,0:T(8,128)} %get-tuple-element.344, f32[2,512]{1,0:T(2,128)S(1)} %get-tuple-element.345), kind=kLoop, calls=%fused_computation.18.clone.1 | loop fusion | flops 4194304 | bytes 12587008 | tf_op jit(solution)/shard_map/while/body/eval_jaxpr/convert_element_type | solution.py:36
  133.1 8.5 %fusion.106 = (f32[2,512]{1,0:T(2,128)S(1)}, f32[2,512,2048]{2,1,0:T(8,128)}) fusion(pred[512,2048]{1,0:T(8,128)(4,1)S(1)} %fusion.105, bf16[2048,128]{1,0:T(8,128)(2,1)} %get-tuple-element.385, bf16[4,512,2,128]{3,1,0,2:T(8,128)(2,1)} %get-tuple-element.384, s32[]{:T(128)S(6)} %copy.179), kind=kOutput, calls=%fused_computation.64.clone.1 | convolution fusion | flops 547358720 | bytes 11276292 | tf_op jit(solution)/shard_map/while/body/eval_jaxpr/sub | solution.py:34
  141.6 4.8 %fusion.107 = bf16[2,512,2048]{2,1,0:T(8,128)(2,1)S(1)} fusion(f32[2,512,2048]{2,1,0:T(8,128)} %get-tuple-element.344, f32[2,512]{1,0:T(2,128)S(1)} %get-tuple-element.345), kind=kLoop, calls=%fused_computation.18.clone.1 | loop fusion | flops 4194304 | bytes 12587008 | tf_op jit(solution)/shard_map/while/body/eval_jaxpr/convert_element_type | solution.py:36
  157.7 8.5 %fusion.106 = (f32[2,512]{1,0:T(2,128)S(1)}, f32[2,512,2048]{2,1,0:T(8,128)}) fusion(pred[512,2048]{1,0:T(8,128)(4,1)S(1)} %fusion.105, bf16[2048,128]{1,0:T(8,128)(2,1)} %get-tuple-element.385, bf16[4,512,2,128]{3,1,0,2:T(8,128)(2,1)} %get-tuple-element.384, s32[]{:T(128)S(6)} %copy.179), kind=kOutput, calls=%fused_computation.64.clone.1 | convolution fusion | flops 547358720 | bytes 11276292 | tf_op jit(solution)/shard_map/while/body/eval_jaxpr/sub | solution.py:34
  182.8 31.2 %all_to_all.105 = f32[2048,1,256]{2,1,0:T(1,128)S(1)} all-to-all(f32[2048,1,256]{2,1,0:T(1,128)S(1)} %reshape.176), channel_id=1, replica_groups=mesh['dp'=8,'seq'=16] {'seq'}, dimensions={0} | all-to-all | bytes 4194304 | tf_op jit(solution)/shard_map/all_to_all | solution.py:116
  218.2 42.4 %all_to_all.106 = bf16[128,8,1024]{0,2,1:T(8,128)(2,1)S(1)} all-to-all(bf16[128,8,1024]{0,2,1:T(8,128)(2,1)} %bitcast.200), channel_id=1, replica_groups=mesh['dp'=8,'seq'=16] {'dp'}, dimensions={1} | all-to-all | bytes 4194304 | tf_op jit(solution)/shard_map/all_to_all | solution.py:130
  263.1 6.5 %multiply_bitcast_fusion = f32[1024,1024]{0,1:T(8,128)} fusion(bf16[1024,1024]{0,1:T(8,128)(2,1)} %all-gather.2.cloned.1.call-done, bf16[1024,1024]{1,0:T(8,128)(2,1)} %bitcast.211), kind=kOutput, calls=%fused_computation.56 | convolution fusion | flops 2148532224 | bytes 8388608 | tf_op jit(solution)/shard_map/dot_general | solution.py:134
  269.6 5.4 %copy.163 = f32[1024,1024]{1,0:T(8,128)} copy(f32[1024,1024]{0,1:T(8,128)} %multiply_bitcast_fusion) | data formatting | bytes 8388608
  276.2 9.4 %copy.146 = bf16[2048,2,128]{2,1,0:T(2,128)(2,1)} copy(bf16[2048,2,128]{2,0,1:T(8,128)(2,1)S(1)} %bitcast.213) | data formatting | bytes 2097152 | tf_op jit(solution)/shard_map/reshape | solution.py:71
  289.5 9.5 %copy.142 = bf16[2048,2,128]{2,1,0:T(2,128)(2,1)} copy(bf16[2048,2,128]{2,0,1:T(8,128)(2,1)S(1)} %bitcast.214) | data formatting | bytes 2097152 | tf_op jit(solution)/shard_map/reshape | solution.py:70
  299.0 10.1 %all-to-all-done.4 = bf16[2048,2,128]{2,1,0:T(2,128)(2,1)S(1)} async-done(((bf16[2048,2,128]{2,1,0:T(2,128)(2,1)}), bf16[2048,2,128]{2,1,0:T(2,128)(2,1)S(1)}, u32[]{:S(2)}, u32[]{:S(2)}) %all-to-all-start.4) | async-done | bytes 1048608 | tf_op jit(solution)/shard_map/all_to_all | solution.py:114
  315.3 16.6 %all-to-all-done.3 = bf16[2048,2,128]{2,1,0:T(2,128)(2,1)S(1)} async-done(((bf16[2048,2,128]{2,1,0:T(2,128)(2,1)}), bf16[2048,2,128]{2,1,0:T(2,128)(2,1)S(1)}, u32[]{:S(2)}, u32[]{:S(2)}) %all-to-all-start.3) | async-done | bytes 1048608 | tf_op jit(solution)/shard_map/all_to_all | solution.py:113
  334.0 12.8 %convolution_convert_fusion.2 = bf16[128,8192]{1,0:T(8,128)(2,1)} fusion(bf16[128,1024]{0,1:T(8,128)(2,1)S(1)} %bitcast.210, bf16[8192,1024]{1,0:T(8,128)(2,1)} %param.10), kind=kOutput, calls=%fused_computation.55 | convolution fusion | flops 2148532224 | bytes 19136512 | tf_op jit(solution)/shard_map/tc,dc->td/dot_general | solution.py:127
  346.9 17.0 %reduce-scatter.4.cloned.1.call-done = f32[64,1024]{1,0:T(8,128)} async-done(((f32[1024,1024]{1,0:T(8,128)}), f32[64,1024]{1,0:T(8,128)}) %reduce-scatter.4.cloned.1.call-update) | async-done | bytes 262160
  (130 shorter events, 90.1 us)
Async XLA Ops:
  16.6 10.0 %copy-start.4 = (bf16[128,4096]{1,0:T(8,128)(2,1)S(1)}, bf16[128,4096]{1,0:T(8,128)(2,1)}, u32[]{:S(2)}) copy-start(bf16[128,4096]{1,0:T(8,128)(2,1)} %param.9) | copy-start | bytes 3145732
  18.0 24.1 %all-to-all-start.1 = ((bf16[128,16,256]{0,2,1:T(8,128)(2,1)}), bf16[128,16,256]{0,2,1:T(8,128)(2,1)S(1)}, u32[]{:S(2)}, u32[]{:S(2)}) async-start(bf16[128,16,256]{0,2,1:T(8,128)(2,1)} %bitcast.10), calls=%async_computation.1 | async-start | bytes 2097152 | tf_op jit(solution)/shard_map/all_to_all | solution.py:105
  26.6 39.2 %copy-start.9 = (s32[1,8]{1,0:T(1,128)S(1)}, s32[1,8]{1,0:T(1,128)}, u32[]{:S(2)}) copy-start(s32[1,8]{1,0:T(1,128)} %param.13) | copy-start | bytes 100
  42.1 18.3 %all-to-all-start = ((bf16[128,32,128]{0,2,1:T(8,128)(2,1)}), bf16[128,32,128]{0,2,1:T(8,128)(2,1)S(1)}, u32[]{:S(2)}, u32[]{:S(2)}) async-start(bf16[128,32,128]{0,2,1:T(8,128)(2,1)} %bitcast.2), calls=%async_computation | async-start | bytes 2097152 | tf_op jit(solution)/shard_map/all_to_all | solution.py:87
  60.4 5.3 %copy-start.2 = (bf16[128,32,128]{0,2,1:T(8,128)(2,1)}, bf16[128,32,128]{0,2,1:T(8,128)(2,1)S(1)}, u32[]{:S(2)}) copy-start(bf16[128,32,128]{0,2,1:T(8,128)(2,1)S(1)} %all-to-all-done) | copy-start | bytes 3145732
  60.4 19.7 %all-to-all-start.2 = ((bf16[128,32,128]{0,2,1:T(8,128)(2,1)}), bf16[128,32,128]{0,2,1:T(8,128)(2,1)}, u32[]{:S(2)}, u32[]{:S(2)}) async-start(bf16[128,32,128]{0,2,1:T(8,128)(2,1)} %bitcast.14), calls=%async_computation.2 | async-start | bytes 2097152 | tf_op jit(solution)/shard_map/all_to_all | solution.py:88
  65.7 197.4 %all-gather.2.cloned.1.call-start = ((), (), s32[]{:S(2)}) async-start(), calls=%async_computation.8 | async-start | bytes 2359296 | tf_op jit(solution)/shard_map/all_gather | solution.py:133
  92.5 4.8 %copy-start.1 = (bf16[4,512,2,128]{3,1,0,2:T(8,128)(2,1)S(1)}, bf16[4,512,2,128]{3,1,0,2:T(8,128)(2,1)}, u32[]{:S(2)}) copy-start(bf16[4,512,2,128]{3,1,0,2:T(8,128)(2,1)} %get-tuple-element.386) | copy-start | bytes 3145732 | tf_op jit(solution)/shard_map/while
  92.5 4.8 %copy-start.7 = (bf16[2048,128]{0,1:T(8,128)(2,1)S(1)}, bf16[2048,128]{0,1:T(8,128)(2,1)}, u32[]{:S(2)}) copy-start(bf16[2048,128]{0,1:T(8,128)(2,1)} %get-tuple-element.387) | copy-start | bytes 1572868 | tf_op jit(solution)/shard_map/while
  92.5 7.7 %slice-start = ((s8[8388608]{0:T(1024)(128)(4,1)}), s8[4194304]{0:T(1024)(128)(4,1)S(1)}, s32[]{:S(2)}) async-start(s8[8388608]{0:T(1024)(128)(4,1)} %bitcast.195), calls=%async_computation.10 | async-start | bytes 8388608 | tf_op jit(solution)/shard_map/while
  117.1 4.8 %copy-start.1 = (bf16[4,512,2,128]{3,1,0,2:T(8,128)(2,1)S(1)}, bf16[4,512,2,128]{3,1,0,2:T(8,128)(2,1)}, u32[]{:S(2)}) copy-start(bf16[4,512,2,128]{3,1,0,2:T(8,128)(2,1)} %get-tuple-element.386) | copy-start | bytes 3145732 | tf_op jit(solution)/shard_map/while
  117.1 4.8 %copy-start.7 = (bf16[2048,128]{0,1:T(8,128)(2,1)S(1)}, bf16[2048,128]{0,1:T(8,128)(2,1)}, u32[]{:S(2)}) copy-start(bf16[2048,128]{0,1:T(8,128)(2,1)} %get-tuple-element.387) | copy-start | bytes 1572868 | tf_op jit(solution)/shard_map/while
  117.1 7.7 %slice-start = ((s8[8388608]{0:T(1024)(128)(4,1)}), s8[4194304]{0:T(1024)(128)(4,1)S(1)}, s32[]{:S(2)}) async-start(s8[8388608]{0:T(1024)(128)(4,1)} %bitcast.195), calls=%async_computation.10 | async-start | bytes 8388608 | tf_op jit(solution)/shard_map/while
  141.6 4.8 %copy-start.1 = (bf16[4,512,2,128]{3,1,0,2:T(8,128)(2,1)S(1)}, bf16[4,512,2,128]{3,1,0,2:T(8,128)(2,1)}, u32[]{:S(2)}) copy-start(bf16[4,512,2,128]{3,1,0,2:T(8,128)(2,1)} %get-tuple-element.386) | copy-start | bytes 3145732 | tf_op jit(solution)/shard_map/while
  141.6 4.8 %copy-start.7 = (bf16[2048,128]{0,1:T(8,128)(2,1)S(1)}, bf16[2048,128]{0,1:T(8,128)(2,1)}, u32[]{:S(2)}) copy-start(bf16[2048,128]{0,1:T(8,128)(2,1)} %get-tuple-element.387) | copy-start | bytes 1572868 | tf_op jit(solution)/shard_map/while
  141.6 7.7 %slice-start = ((s8[8388608]{0:T(1024)(128)(4,1)}), s8[4194304]{0:T(1024)(128)(4,1)S(1)}, s32[]{:S(2)}) async-start(s8[8388608]{0:T(1024)(128)(4,1)} %bitcast.195), calls=%async_computation.10 | async-start | bytes 8388608 | tf_op jit(solution)/shard_map/while
  166.2 4.8 %copy-start.1 = (bf16[4,512,2,128]{3,1,0,2:T(8,128)(2,1)S(1)}, bf16[4,512,2,128]{3,1,0,2:T(8,128)(2,1)}, u32[]{:S(2)}) copy-start(bf16[4,512,2,128]{3,1,0,2:T(8,128)(2,1)} %get-tuple-element.386) | copy-start | bytes 3145732 | tf_op jit(solution)/shard_map/while
  166.2 4.8 %copy-start.7 = (bf16[2048,128]{0,1:T(8,128)(2,1)S(1)}, bf16[2048,128]{0,1:T(8,128)(2,1)}, u32[]{:S(2)}) copy-start(bf16[2048,128]{0,1:T(8,128)(2,1)} %get-tuple-element.387) | copy-start | bytes 1572868 | tf_op jit(solution)/shard_map/while
  166.2 7.7 %slice-start = ((s8[8388608]{0:T(1024)(128)(4,1)}), s8[4194304]{0:T(1024)(128)(4,1)S(1)}, s32[]{:S(2)}) async-start(s8[8388608]{0:T(1024)(128)(4,1)} %bitcast.195), calls=%async_computation.10 | async-start | bytes 8388608 | tf_op jit(solution)/shard_map/while
  215.2 148.6 %reduce-scatter.4.cloned.1.call-start = ((), (), s32[]{:S(2)}) async-start(), calls=%async_computation.9 | async-start | bytes 4456448
  275.0 14.5 %copy-start.6 = (bf16[4,512,2,128]{3,1,0,2:T(8,128)(2,1)S(1)}, bf16[4,512,2,128]{3,1,0,2:T(8,128)(2,1)}, u32[]{:S(2)}) copy-start(bf16[4,512,2,128]{3,1,0,2:T(8,128)(2,1)} %get-tuple-element.74) | copy-start | bytes 3145732
  285.6 23.4 %all-to-all-start.4 = ((bf16[2048,2,128]{2,1,0:T(2,128)(2,1)}), bf16[2048,2,128]{2,1,0:T(2,128)(2,1)S(1)}, u32[]{:S(2)}, u32[]{:S(2)}) async-start(bf16[2048,2,128]{2,1,0:T(2,128)(2,1)} %copy.146), calls=%async_computation.4 | async-start | bytes 2097152 | tf_op jit(solution)/shard_map/all_to_all | solution.py:114
  309.0 22.9 %all-to-all-start.3 = ((bf16[2048,2,128]{2,1,0:T(2,128)(2,1)}), bf16[2048,2,128]{2,1,0:T(2,128)(2,1)S(1)}, u32[]{:S(2)}, u32[]{:S(2)}) async-start(bf16[2048,2,128]{2,1,0:T(2,128)(2,1)} %copy.142), calls=%async_computation.3 | async-start | bytes 2097152 | tf_op jit(solution)/shard_map/all_to_all | solution.py:113
  314.0 20.1 %copy-start.3 = (bf16[128,4,256]{0,2,1:T(8,128)(2,1)S(1)}, bf16[128,4,256]{0,2,1:T(8,128)(2,1)}, u32[]{:S(2)}) copy-start(bf16[128,4,256]{0,2,1:T(8,128)(2,1)} %copy.149) | copy-start | bytes 786436
  (10 other events, 24.8 us)
Sparse Core Ops, SparseCore 0:
  215.4 42.4 all-gather.1
  275.1 88.6 reduce-scatter.3

commit v2 on v0

v2 whole, which is shorter than its diff:
```python
import functools
import math

import jax
import jax.numpy as jnp
from jax import lax
from jax.experimental import pallas as pl
from jax.experimental.pallas import tpu as pltpu
from jax.sharding import PartitionSpec as P

GROUPS = 4
GROUP_HEADS = 8
HEAD = 128
PAIR = 2 * HEAD
TOK = 128
BACK = 8
SLOTS = BACK + 1
KEYS = SLOTS * TOK
D = 8192
N_DP = 8
N_SEQ = 16
D_PART = D // N_DP
D_OWN = D_PART // N_SEQ
SCALE = 1.0 / math.sqrt(HEAD)
LOG2E = 1.4426950408889634
FACTOR = 1.0 / math.sqrt(TOK * N_DP * N_SEQ)
F32 = jnp.float32
BF16 = jnp.bfloat16


def dot(a, b):
    return jnp.dot(a, b, preferred_element_type=F32)


def kernel(
    hidden_hbm, queries_hbm, weight_hbm, bias_ref, cot_hbm, lengths_ref,
    att_hbm, qgrad_hbm, hgrad_hbm, wgrad_hbm,
    hid, qry, cot, wgt, kv, mask, kt, vt, acc, att, qgr, hgr, wgr,
    dk_out, dk_in, dk_own, dkv, dkvt, hx, hxt, dall, w_out, w_in,
    in_sem, wgt_sem, kv_s, kv_r, dk_s, dk_r, hx_s, hx_r, ag_s, ag_r, rs_s, rs_r, out_sem,
):
    me = lax.axis_index("seq")
    row = lax.axis_index("dp")
    before = jnp.minimum(me, BACK)
    after = jnp.minimum(N_SEQ - 1 - me, BACK)

    in_hid = pltpu.make_async_copy(hidden_hbm, hid, in_sem.at[0])
    in_qry = pltpu.make_async_copy(queries_hbm, qry, in_sem.at[1])
    in_cot = pltpu.make_async_copy(cot_hbm, cot, in_sem.at[2])
    in_hid.start()

    def weight_copy(g):
        return pltpu.make_async_copy(
            weight_hbm.at[:, pl.ds(pl.multiple_of(g * PAIR, PAIR), PAIR)], wgt.at[g], wgt_sem.at[g]
        )

    def start_weight(g, _):
        weight_copy(g).start()
        return 0

    lax.fori_loop(0, GROUPS, start_weight, 0)
    in_qry.start()
    in_cot.start()

    barrier = pltpu.get_barrier_semaphore()

    def greet_seq(i, _):
        pl.semaphore_signal(
            barrier, inc=1, device_id={"seq": lax.rem(me + 1 + i, N_SEQ)},
            device_id_type=pl.DeviceIdType.MESH,
        )
        return 0

    def greet_dp(i, _):
        pl.semaphore_signal(
            barrier, inc=1, device_id={"dp": lax.rem(row + 1 + i, N_DP)},
            device_id_type=pl.DeviceIdType.MESH,
        )
        return 0

    lax.fori_loop(0, N_SEQ - 1, greet_seq, 0)
    lax.fori_loop(0, N_DP - 1, greet_dp, 0)

    p_pos = me * TOK + lax.broadcasted_iota(jnp.int32, (1, TOK), 1)
    start = jnp.zeros((1, TOK), jnp.int32)
    end = jnp.int32(0)
    for i in range(lengths_ref.shape[1]):
        end = end + lengths_ref[0, i]
        start = jnp.where(p_pos >= end, end, start)
    k_pos = (me - BACK) * TOK + lax.broadcasted_iota(jnp.int32, (KEYS, TOK), 0)
    mask[...] = jnp.where((k_pos >= start) & (k_pos <= p_pos), 0.0, -1e30).astype(F32)

    def clear(s, _):
        for g in range(GROUPS):
            kv[g, pl.ds(pl.multiple_of(s * TOK, TOK), TOK), :] = jnp.zeros((TOK, PAIR), BF16)
        return 0

    lax.fori_loop(0, BACK - before, clear, 0)

    in_hid.wait()
    pl.semaphore_wait(barrier, N_SEQ - 1 + N_DP - 1)

    def hx_copy(i):
        peer = lax.rem(row + 1 + i, N_DP)
        return pltpu.make_async_remote_copy(
            src_ref=hid.at[:, pl.ds(pl.multiple_of(peer * D_PART, D_PART), D_PART)],
            dst_ref=hx.at[pl.ds(pl.multiple_of(row * TOK, TOK), TOK), :],
            send_sem=hx_s.at[i],
            recv_sem=hx_r.at[row],
            device_id={"dp": peer},
            device_id_type=pl.DeviceIdType.MESH,
        )

    hx_own = pltpu.make_async_copy(
        hid.at[:, pl.ds(pl.multiple_of(row * D_PART, D_PART), D_PART)],
        hx.at[pl.ds(pl.multiple_of(row * TOK, TOK), TOK), :],
        in_sem.at[3],
    )

    def kv_copy(g, d):
        return pltpu.make_async_remote_copy(
            src_ref=kv.at[g, pl.ds(BACK * TOK, TOK), :],
            dst_ref=kv.at[g, pl.ds(pl.multiple_of((BACK - 1 - d) * TOK, TOK), TOK), :],
            send_sem=kv_s.at[g, d],
            recv_sem=kv_r.at[g, BACK - 1 - d],
            device_id={"seq": jnp.minimum(me + 1 + d, N_SEQ - 1)},
            device_id_type=pl.DeviceIdType.MESH,
        )

    def project(g, _):
        weight_copy(g).wait()

        def step(i, total):
            cols = pl.ds(pl.multiple_of(i * 1024, 1024), 1024)
            return total + dot(hid[:, cols], wgt[g, cols, :])

        total = lax.fori_loop(0, D // 1024, step, jnp.zeros((TOK, PAIR), F32))
        kv[g, BACK * TOK :, :HEAD] = total[:, :HEAD].astype(BF16)
        kv[g, BACK * TOK :, HEAD:] = (total[:, HEAD:] + bias_ref[g]).astype(BF16)

        def send(d, _):
            kv_copy(g, d).start()
            return 0

        lax.fori_loop(0, after, send, 0)
        return 0

    lax.fori_loop(0, GROUPS, project, 0)

    def start_hx(i, _):
        hx_copy(i).start()
        return 0

    lax.fori_loop(0, N_DP - 1, start_hx, 0)
    hx_own.start()
    in_qry.wait()
    in_cot.wait()

    def dk_copy(g, d):
        return pltpu.make_async_remote_copy(
            src_ref=dk_out.at[g, pl.ds(pl.multiple_of((BACK - 1 - d) * TOK, TOK), TOK), :],
            dst_ref=dk_in.at[g, d],
            send_sem=dk_s.at[g, d],
            recv_sem=dk_r.at[g, d],
            device_id={"seq": jnp.maximum(me - 1 - d, 0)},
            device_id_type=pl.DeviceIdType.MESH,
        )

    def att_copy(g):
        cols = pl.ds(pl.multiple_of(g * 1024, 1024), 1024)
        return pltpu.make_async_copy(att.at[:, cols], att_hbm.at[:, cols], out_sem.at[0, g])

    def qgr_copy(g):
        cols = pl.ds(pl.multiple_of(g * 1024, 1024), 1024)
        return pltpu.make_async_copy(qgr.at[:, cols], qgrad_hbm.at[:, cols], out_sem.at[1, g])

    def attention(g):
        def arrive(d, _):
            kv_copy(g, BACK - 1 - (BACK - 1 - d)).wait_recv()
            return 0

        lax.fori_loop(0, before, arrive, 0)
        kt[...] = kv[g, :, :HEAD].T
        vt[...] = kv[g, :, HEAD:].T
        acc[...] = jnp.zeros((KEYS, PAIR), F32)

        def heads(c, _):
            cols = pl.ds(pl.multiple_of(g * 1024 + c * PAIR, PAIR), PAIR)
            q2 = qry[:, cols]
            o2 = cot[:, cols]
            q_rows = jnp.concatenate([q2[:, :HEAD], q2[:, HEAD:]], axis=0)
            o_rows = jnp.concatenate([o2[:, :HEAD], o2[:, HEAD:]], axis=0)
            q_t = jnp.concatenate([q2[:, :HEAD].T, q2[:, HEAD:].T], axis=1)
            o_t = jnp.concatenate([o2[:, :HEAD].T, o2[:, HEAD:].T], axis=1)
            bias = mask[...]
            s = dot(kv[g, :, :HEAD], q_t) + jnp.concatenate([bias, bias], axis=1)
            top = jnp.max(s, axis=0, keepdims=True)
            e = jnp.exp2((s - top) * (SCALE * LOG2E))
            inv = 1.0 / jnp.sum(e, axis=0, keepdims=True)
            prob = e * inv
            half = prob.astype(BF16)
            out_t = dot(vt[...], half)
            out_b = out_t.astype(BF16)
            delta = jnp.sum(o_t.astype(F32) * out_b.astype(F32), axis=0, keepdims=True)
            dp = dot(kv[g, :, HEAD:], o_t)
            ds = (prob * (dp - delta)).astype(BF16)
            dq_t = dot(kt[...], ds) * SCALE
            acc[:, :HEAD] += dot(ds, q_rows)
            acc[:, HEAD:] += dot(half, o_rows)
            att[:, cols] = jnp.concatenate(
                [out_t[:, :HEAD].T, out_t[:, HEAD:].T], axis=1
            ).astype(BF16)
            qgr[:, cols] = jnp.concatenate([dq_t[:, :HEAD].T, dq_t[:, HEAD:].T], axis=1).astype(
                BF16
            )
            return 0

        lax.fori_loop(0, GROUP_HEADS // 2, heads, 0)
        dk_out[g, :, :HEAD] = (acc[: BACK * TOK, :HEAD] * SCALE).astype(BF16)
        dk_out[g, :, HEAD:] = acc[: BACK * TOK, HEAD:].astype(BF16)
        dk_own[g, :, :HEAD] = acc[BACK * TOK :, :HEAD] * SCALE
        dk_own[g, :, HEAD:] = acc[BACK * TOK :, HEAD:]

        def send(d, _):
            dk_copy(g, d).start()
            return 0

        lax.fori_loop(0, before, send, 0)
        att_copy(g).start()
        qgr_copy(g).start()

    def ag_copy(g, i):
        return pltpu.make_async_remote_copy(
            src_ref=dkv.at[g],
            dst_ref=dall.at[g, pl.ds(pl.multiple_of(row * TOK, TOK), TOK), :],
            send_sem=ag_s.at[g, i],
            recv_sem=ag_r.at[g, row],
            device_id={"dp": lax.rem(row + 1 + i, N_DP)},
            device_id_type=pl.DeviceIdType.MESH,
        )

    def home(g):
        def arrive(d, total):
            dk_copy(g, d).wait_recv()
            return total + dk_in[g, d].astype(F32)

        total = lax.fori_loop(0, after, arrive, dk_own[g])
        half = total.astype(BF16)
        dkv[g] = half
        dall[g, pl.ds(pl.multiple_of(row * TOK, TOK), TOK), :] = half
        dkvt[pl.ds(pl.multiple_of(g * PAIR, PAIR), PAIR), :] = half.T

        def send(i, _):
            ag_copy(g, i).start()
            return 0

        lax.fori_loop(0, N_DP - 1, send, 0)

    def hx_arrive():
        def arrive(i, _):
            peer = lax.rem(row + 1 + i, N_DP)
            pltpu.make_async_remote_copy(
                src_ref=hid.at[:, pl.ds(0, D_PART)],
                dst_ref=hx.at[pl.ds(pl.multiple_of(peer * TOK, TOK), TOK), :],
                send_sem=hx_s.at[i],
                recv_sem=hx_r.at[peer],
                device_id={"dp": peer},
                device_id_type=pl.DeviceIdType.MESH,
            ).wait_recv()
            return 0

        lax.fori_loop(0, N_DP - 1, arrive, 0)
        hx_own.wait()

        def turn(i, _):
            rows = pl.ds(pl.multiple_of(i * TOK, TOK), TOK)
            hxt[:, rows] = hx[rows, :].T
            return 0

        lax.fori_loop(0, N_DP, turn, 0)

    def rs_copy(g, i):
        peer = lax.rem(me + 1 + i, N_SEQ)
        return pltpu.make_async_remote_copy(
            src_ref=w_out.at[g, pl.ds(pl.multiple_of(peer * D_OWN, D_OWN), D_OWN), :],
            dst_ref=w_in.at[g, me],
            send_sem=rs_s.at[g, i],
            recv_sem=rs_r.at[g, me],
            device_id={"seq": peer},
            device_id_type=pl.DeviceIdType.MESH,
        )

    def product(g):
        def arrive(i, _):
            peer = lax.rem(row + 1 + i, N_DP)
            pltpu.make_async_remote_copy(
                src_ref=dkv.at[g],
                dst_ref=dall.at[g, pl.ds(pl.multiple_of(peer * TOK, TOK), TOK), :],
                send_sem=ag_s.at[g, i],
                recv_sem=ag_r.at[g, peer],
                device_id={"dp": peer},
                device_id_type=pl.DeviceIdType.MESH,
            ).wait_recv()
            return 0

        lax.fori_loop(0, N_DP - 1, arrive, 0)

        def tile(i, _):
            rows = pl.ds(pl.multiple_of(i * 256, 256), 256)
            w_out[g, rows, :] = dot(hxt[rows, :], dall[g]).astype(BF16)
            return 0

        lax.fori_loop(0, D_PART // 256, tile, 0)

        def send(i, _):
            rs_copy(g, i).start()
            return 0

        lax.fori_loop(0, N_SEQ - 1, send, 0)

    def finish(g):
        own = w_out[g, pl.ds(pl.multiple_of(me * D_OWN, D_OWN), D_OWN), :].astype(F32)

        def arrive(i, total):
            peer = lax.rem(me + 1 + i, N_SEQ)
            pltpu.make_async_remote_copy(
                src_ref=w_out.at[g, pl.ds(0, D_OWN), :],
                dst_ref=w_in.at[g, peer],
                send_sem=rs_s.at[g, i],
                recv_sem=rs_r.at[g, peer],
                device_id={"seq": peer},
                device_id_type=pl.DeviceIdType.MESH,
            ).wait_recv()
            return total + w_in[g, peer].astype(F32)

        total = lax.fori_loop(0, N_SEQ - 1, arrive, own)
        wgr[:, pl.ds(pl.multiple_of(g * PAIR, PAIR), PAIR)] = total * FACTOR

    HG = 512

    def hgr_copy(i):
        cols = pl.ds(pl.multiple_of(i * HG, HG), HG)
        return pltpu.make_async_copy(hgr.at[:, cols], hgrad_hbm.at[:, cols], out_sem.at[2, i])

    def hidden_gradient(i, _):
        cols = pl.ds(pl.multiple_of(i * HG, HG), HG)
        total = dot(wgt[0, cols, :], dkvt[:PAIR, :])
        for g in range(1, GROUPS):
            total = total + dot(wgt[g, cols, :], dkvt[g * PAIR : (g + 1) * PAIR, :])
        hgr[:, cols] = total.T.astype(BF16)
        hgr_copy(i).start()
        return 0

    def stage(t, _):
        @pl.when(t < GROUPS)
        def _():
            attention(t)

        @pl.when((t >= 1) & (t <= GROUPS))
        def _():
            home(t - 1)

        @pl.when(t == 1)
        def _():
            hx_arrive()

        @pl.when(t == GROUPS)
        def _():
            lax.fori_loop(0, D // HG // 2, hidden_gradient, 0)

        @pl.when(t >= 2)
        def _():
            product(t - 2)

        return 0

    lax.fori_loop(0, GROUPS + 2, stage, 0)
    lax.fori_loop(D // HG // 2, D // HG, hidden_gradient, 0)

    def last(g, _):
        finish(g)
        return 0

    lax.fori_loop(0, GROUPS, last, 0)
    wgr_copy = pltpu.make_async_copy(wgr, wgrad_hbm, in_sem.at[4])
    wgr_copy.start()

    def drain(g, _):
        def kv_end(d, _):
            kv_copy(g, d).wait_send()
            return 0

        def dk_end(d, _):
            dk_copy(g, d).wait_send()
            return 0

        def ag_end(i, _):
            ag_copy(g, i).wait_send()
            return 0

        def rs_end(i, _):
            rs_copy(g, i).wait_send()
            return 0

        lax.fori_loop(0, after, kv_end, 0)
        lax.fori_loop(0, before, dk_end, 0)
        lax.fori_loop(0, N_DP - 1, ag_end, 0)
        lax.fori_loop(0, N_SEQ - 1, rs_end, 0)
        att_copy(g).wait()
        qgr_copy(g).wait()
        return 0

    def hx_end(i, _):
        hx_copy(i).wait_send()
        return 0

    def hgr_end(i, _):
        hgr_copy(i).wait()
        return 0

    lax.fori_loop(0, GROUPS, drain, 0)
    lax.fori_loop(0, N_DP - 1, hx_end, 0)
    lax.fori_loop(0, D // HG, hgr_end, 0)
    wgr_copy.wait()


def local(hidden, queries, kv_weight, value_projection_bias, cotangent, lengths):
    any_spec = pl.BlockSpec(memory_space=pl.ANY)
    vmem = pltpu.VMEM
    dma = pltpu.SemaphoreType.DMA
    width = GROUPS * GROUP_HEADS * HEAD
    return pl.pallas_call(
        kernel,
        out_shape=(
            jax.ShapeDtypeStruct((TOK, width), BF16),
            jax.ShapeDtypeStruct((TOK, width), BF16),
            jax.ShapeDtypeStruct((TOK, D), BF16),
            jax.ShapeDtypeStruct((D_OWN, GROUPS * PAIR), F32),
        ),
        in_specs=[
            any_spec,
            any_spec,
            any_spec,
            pl.BlockSpec(memory_space=pltpu.VMEM),
            any_spec,
            pl.BlockSpec(memory_space=pltpu.SMEM),
        ],
        out_specs=(any_spec,) * 4,
        scratch_shapes=[
            vmem((TOK, D), BF16),
            vmem((TOK, width), BF16),
            vmem((TOK, width), BF16),
            vmem((GROUPS, D, PAIR), BF16),
            vmem((GROUPS, KEYS, PAIR), BF16),
            vmem((KEYS, TOK), F32),
            vmem((HEAD, KEYS), BF16),
            vmem((HEAD, KEYS), BF16),
            vmem((KEYS, PAIR), F32),
            vmem((TOK, width), BF16),
            vmem((TOK, width), BF16),
            vmem((TOK, D), BF16),
            vmem((D_OWN, GROUPS * PAIR), F32),
            vmem((GROUPS, BACK * TOK, PAIR), BF16),
            vmem((GROUPS, BACK, TOK, PAIR), BF16),
            vmem((GROUPS, TOK, PAIR), F32),
            vmem((GROUPS, TOK, PAIR), BF16),
            vmem((GROUPS * PAIR, TOK), BF16),
            vmem((N_DP * TOK, D_PART), BF16),
            vmem((D_PART, N_DP * TOK), BF16),
            vmem((GROUPS, N_DP * TOK, PAIR), BF16),
            vmem((GROUPS, D_PART, PAIR), BF16),
            vmem((GROUPS, N_SEQ, D_OWN, PAIR), BF16),
            dma((5,)),
            dma((GROUPS,)),
            dma((GROUPS, BACK)),
            dma((GROUPS, BACK)),
            dma((GROUPS, BACK)),
            dma((GROUPS, BACK)),
            dma((N_DP,)),
            dma((N_DP,)),
            dma((GROUPS, N_DP)),
            dma((GROUPS, N_DP)),
            dma((GROUPS, N_SEQ)),
            dma((GROUPS, N_SEQ)),
            dma((3, 16)),
        ],
        compiler_params=pltpu.CompilerParams(
            collective_id=0, has_side_effects=True, vmem_limit_bytes=60 * 1024 * 1024
        ),
        cost_estimate=pl.CostEstimate(
            flops=14_000_000_000, bytes_accessed=26_000_000, transcendentals=5_000_000
        ),
    )(
        hidden,
        queries,
        kv_weight,
        value_projection_bias.reshape(GROUPS, 1, HEAD),
        cotangent,
        lengths,
    )


def solution(mesh):
    both = P(("dp", "seq"), None)
    return jax.shard_map(
        local,
        mesh=mesh,
        in_specs=(both, both, P(), P(), both, P("dp", None)),
        out_specs=(both,) * 4,
        check_vma=False,
    )
```

time: 1010 us -> 119 us (0.12)
  the two profiles are of different devices: /device:TPU:0 before, /device:TPU:1 now
where the time goes in v2:
time: 119 us
  Pallas kernels  113 us (95%)
  local copies, waits for them, and re-layouts  5.44 us (5%)
    pallas_call x1, Pallas kernels, local(): pl.pallas_call(kernel, out_shape=(jax.ShapeDtypeStruct((TOK, width), BF16...  113 us
    unnamed x10, local copies, waits for them, and re-layouts  5.44 us

profile of v2, /device:TPU:1, one launch (start us, length us, event | category | flops | bytes accessed | tf_op | source)
XLA Modules:
  0.0 119.0 jit_solution(3157678896060909496)
XLA Ops:
  0.6 112.9 %shard_map.93 = (bf16[128,4096]{1,0:T(8,128)(2,1)}, bf16[128,4096]{1,0:T(8,128)(2,1)}, bf16[128,8192]{1,0:T(8,128)(2,1)}, f32[64,1024]{1,0:T(8,128)}) custom-call(bf16[128,8192]{1,0:T(8,128)(2,1)} %hidden_hbm.1, bf16[128,4096]{1,0:T(8,128)(2,1)} %queries_hbm.1, bf16[8192,1024]{1,0:T(8,128)(2,1)} %weight_hbm.1, f32[4,1,128]{2,1,0:T(1,128)} %bitcast.1, ...), custom_call_target="tpu_custom_call" | custom-call | flops 14000000000 | bytes 26000000 | tf_op jit(solution)/shard_map/pallas_call | solution.py:432
  113.5 0.0 copy-start.1
  113.5 0.0 copy-start
  113.5 2.4 %copy.14 = bf16[128,4096]{1,0:T(8,128)(2,1)} copy(bf16[128,4096]{1,0:T(8,128)(2,1)} %get-tuple-element.8) | data formatting | bytes 2097152
  116.0 0.0 copy-done.1
  116.0 1.0 copy.15
  116.9 0.0 copy-done
  116.9 0.0 copy-start.2
  116.9 1.3 %copy.16 = bf16[128,8192]{1,0:T(8,128)(2,1)} copy(bf16[128,8192]{1,0:T(8,128)(2,1)S(1)} %copy-done) | data formatting | bytes 4194304
  118.2 0.0 copy-done.2
  118.3 0.7 copy.17
Async XLA Ops:
  113.5 2.5 %copy-start.1 = (bf16[128,4096]{1,0:T(8,128)(2,1)S(1)}, bf16[128,4096]{1,0:T(8,128)(2,1)}, u32[]{:S(2)}) copy-start(bf16[128,4096]{1,0:T(8,128)(2,1)} %get-tuple-element.9) | copy-start | bytes 3145732
  113.5 3.4 %copy-start = (bf16[128,8192]{1,0:T(8,128)(2,1)S(1)}, bf16[128,8192]{1,0:T(8,128)(2,1)}, u32[]{:S(2)}) copy-start(bf16[128,8192]{1,0:T(8,128)(2,1)} %get-tuple-element.10) | copy-start | bytes 6291460
  116.9 1.3 %copy-start.2 = (f32[64,1024]{1,0:T(8,128)S(1)}, f32[64,1024]{1,0:T(8,128)}, u32[]{:S(2)}) copy-start(f32[64,1024]{1,0:T(8,128)} %get-tuple-element.11) | copy-start | bytes 786436

commit v3 on v2

v3 whole, which is shorter than its diff:
```python
import functools
import math

import jax
import jax.numpy as jnp
from jax import lax
from jax.experimental import pallas as pl
from jax.experimental.pallas import tpu as pltpu
from jax.sharding import PartitionSpec as P

GROUPS = 4
GROUP_HEADS = 8
HEAD = 128
PAIR = 2 * HEAD
TOK = 128
BACK = 8
SLOTS = BACK + 1
KEYS = SLOTS * TOK
D = 8192
N_DP = 8
N_SEQ = 16
D_PART = D // N_DP
D_OWN = D_PART // N_SEQ
SIDE = 4
BLOCK = 3 * TOK
HG = 2048
SCALE = 1.0 / math.sqrt(HEAD)
LOG2E = 1.4426950408889634
FACTOR = 1.0 / math.sqrt(TOK * N_DP * N_SEQ)
F32 = jnp.float32
BF16 = jnp.bfloat16


def dot(a, b):
    return jnp.dot(a, b, preferred_element_type=F32)


def kernel(
    hidden_hbm, queries_hbm, weight_hbm, bias_ref, cot_hbm, lengths_ref,
    att_hbm, qgrad_hbm, hgrad_hbm, wgrad_hbm,
    hid, qry, cot, wgt, kv, mask, kt, vt, q_rows, o_rows, o_cols, delta, prob, dscore, att, qgr, hgr, hgr_sum, wgr,
    dk_out, dk_in, dk_sum, dk_row, dk_col, dk_own, dkvt, hx, hxt, dall,
    w_out, w_in,
    in_sem, wgt_sem, kv_s, kv_r, dk_s, dk_r, dc_s, dc_r, hx_s, hx_r, ag_s, ag_r,
    rs_s, rs_r, out_sem,
):
    me = lax.axis_index("seq")
    row = lax.axis_index("dp")
    y, z = me // SIDE, lax.rem(me, SIDE)

    def remote(src, dst, send, recv, **peer):
        return pltpu.make_async_remote_copy(
            src_ref=src, dst_ref=dst, send_sem=send, recv_sem=recv, device_id=peer,
            device_id_type=pl.DeviceIdType.MESH,
        )

    def part(index, size):
        return pl.ds(pl.multiple_of(index * size, size), size)

    def each(count, body):
        def step(i, _):
            body(i)
            return 0

        lax.fori_loop(0, count, step, 0)

    def other(mine, i, count):
        return lax.rem(mine + 1 + i, count)

    def go(copy, wait):
        if wait:
            copy.wait_send()
        else:
            copy.start()

    in_hid = pltpu.make_async_copy(hidden_hbm, hid, in_sem.at[0])
    in_qry = pltpu.make_async_copy(queries_hbm, qry, in_sem.at[1])
    in_cot = pltpu.make_async_copy(cot_hbm, cot, in_sem.at[2])
    in_hid.start()

    def weight_copy(g):
        return pltpu.make_async_copy(weight_hbm.at[:, part(g, PAIR)], wgt.at[g], wgt_sem.at[g])

    weight_copy(0).start()
    weight_copy(1).start()

    barrier = pltpu.get_barrier_semaphore()

    def greet(**peer):
        pl.semaphore_signal(
            barrier, inc=1, device_id=peer, device_id_type=pl.DeviceIdType.MESH
        )

    each(N_SEQ - 1, lambda i: greet(seq=other(me, i, N_SEQ)))
    each(N_DP - 1, lambda i: greet(dp=other(row, i, N_DP)))

    p_pos = me * TOK + lax.broadcasted_iota(jnp.int32, (1, TOK), 1)
    start = jnp.zeros((1, TOK), jnp.int32)
    end = jnp.int32(0)
    for i in range(lengths_ref.shape[1]):
        end = end + lengths_ref[0, i]
        start = jnp.where(p_pos >= end, end, start)
    k_pos = (me - BACK) * TOK + lax.broadcasted_iota(jnp.int32, (KEYS, TOK), 0)
    mask[...] = jnp.where((k_pos >= start) & (k_pos <= p_pos), 0.0, -1e30).astype(F32)

    def clear(s):
        for g in range(GROUPS):
            kv[g, part(s, TOK), :] = jnp.zeros((TOK, PAIR), BF16)

    each(jnp.maximum(BACK - me, 0), clear)

    in_hid.wait()
    pl.semaphore_wait(barrier, N_SEQ - 1 + N_DP - 1)

    def kv_send(g, message, src, dst, peer):
        return remote(
            kv.at[g, part(src, TOK), :], kv.at[g, part(dst, TOK), :],
            kv_s.at[g, message], kv_r.at[g, dst], seq=peer,
        )

    def along_z(g, i, first, slot, wait):
        to = other(z, i, SIDE)
        dst = jnp.clip(slot + z - to, 0, BACK - 1)
        go(kv_send(g, first + i, slot, dst, y * SIDE + to), wait)

    def kv_first(g, wait=False):
        for rows in (1, 2):
            @pl.when(y + rows < SIDE)
            def _():
                to = jnp.minimum(me + SIDE * rows, N_SEQ - 1)
                go(kv_send(g, rows - 1, BACK, BACK - SIDE * rows, to), wait)

        def own(i):
            @pl.when(other(z, i, SIDE) > z)
            def _():
                along_z(g, i, 2, BACK, wait)

        each(SIDE - 1, own)

    def kv_arrive(g, s):
        kv_send(g, 0, BACK, s, me).wait_recv()

    def kv_second(g, wait=False):
        @pl.when(y >= 1)
        def _():
            if not wait:
                kv_arrive(g, SIDE)
            each(SIDE - 1, lambda i: along_z(g, i, 5, SIDE, wait))

        @pl.when(y >= 2)
        def _():
            if not wait:
                kv_arrive(g, 0)

            def two_before(i):
                @pl.when(other(z, i, SIDE) < z)
                def _():
                    along_z(g, i, 8, 0, wait)

            each(SIDE - 1, two_before)

    def kv_rest(g):
        def arrive(s):
            @pl.when((lax.rem(s, SIDE) != 0) & (me + s >= BACK))
            def _():
                kv_arrive(g, s)

        each(BACK, arrive)

    def project(g):
        weight_copy(g).wait()

        @pl.when(g + 2 < GROUPS)
        def _():
            weight_copy(g + 2).start()

        def step(i, total):
            cols = part(i, 2048)
            return total + dot(hid[:, cols], wgt[g, cols, :])

        total = lax.fori_loop(0, D // 2048, step, jnp.zeros((TOK, PAIR), F32))
        kv[g, BACK * TOK :, :HEAD] = total[:, :HEAD].astype(BF16)
        kv[g, BACK * TOK :, HEAD:] = (total[:, HEAD:] + bias_ref[g]).astype(BF16)

    def hx_copy(i, slot, peer):
        return remote(
            hid.at[:, part(peer, D_PART)], hx.at[part(slot, TOK), :],
            hx_s.at[i], hx_r.at[slot], dp=peer,
        )

    hx_own = pltpu.make_async_copy(
        hid.at[:, part(row, D_PART)], hx.at[part(row, TOK), :], in_sem.at[3]
    )
    def prepare(t):
        project(t)

        kv_first(t)

        @pl.when(t == 0)
        def _():
            each(N_DP - 1, lambda i: hx_copy(i, row, other(row, i, N_DP)).start())
            hx_own.start()
            in_qry.start()
            in_cot.start()

        @pl.when(t >= 2)
        def _():
            kv_second(t - 2)

    each(GROUPS, prepare)
    kv_second(2)
    in_qry.wait()
    in_cot.wait()

    def hx_arrive():
        def arrive(i):
            peer = other(row, i, N_DP)
            hx_copy(i, peer, peer).wait_recv()

        each(N_DP - 1, arrive)
        hx_own.wait()

        def turn(i):
            hxt[:, part(i, TOK)] = hx[part(i, TOK), :].T

        each(N_DP, turn)

    def att_copy(g):
        cols = part(g, 1024)
        return pltpu.make_async_copy(att.at[:, cols], att_hbm.at[:, cols], out_sem.at[0, g])

    def qgr_copy(g):
        cols = part(g, 1024)
        return pltpu.make_async_copy(qgr.at[:, cols], qgrad_hbm.at[:, cols], out_sem.at[1, g])

    WIDE = GROUP_HEADS * HEAD

    def stacked(wide):
        return jnp.concatenate([wide[:, h * HEAD : (h + 1) * HEAD] for h in range(GROUP_HEADS)], 0)

    def turned(wide):
        return jnp.concatenate([wide[:, h * HEAD : (h + 1) * HEAD].T for h in range(GROUP_HEADS)], 1)

    def forward(g):
        kt[...] = kv[g, :, :HEAD].T
        vt[...] = kv[g, :, HEAD:].T
        cols = part(g, WIDE)
        q_wide = qry[:, cols]
        o_wide = cot[:, cols]
        q_rows[...] = stacked(q_wide)
        o_rows[...] = stacked(o_wide)
        turned_o = turned(o_wide)
        o_cols[...] = turned_o
        s = dot(kv[g, :, :HEAD], turned(q_wide)) + jnp.concatenate([mask[...]] * GROUP_HEADS, 1)
        top = jnp.max(s, axis=0, keepdims=True)
        e = jnp.exp2((s - top) * (SCALE * LOG2E))
        inv = 1.0 / jnp.sum(e, axis=0, keepdims=True)
        half = (e * inv).astype(BF16)
        prob[...] = half
        out = dot(vt[...], half)
        out_b = out.astype(BF16).astype(F32)
        delta[...] = jnp.sum(turned_o.astype(F32) * out_b, axis=0, keepdims=True)
        att[:, cols] = turned(out).astype(BF16)
        att_copy(g).start()

    def backward(g, b):
        rows = part(b, BLOCK)
        half = prob[rows, :]
        dp = dot(kv[g, rows, HEAD:], o_cols[...])
        ds = (half.astype(F32) * (dp - delta[...])).astype(BF16)
        dscore[rows, :] = ds
        dk = dot(ds, q_rows[...]) * SCALE
        dv = dot(half, o_rows[...])
        dk_out[g, rows, :HEAD] = dk.astype(BF16)
        dk_out[g, rows, HEAD:] = dv.astype(BF16)
        dk_own[g, :, :HEAD] = dk[BLOCK - TOK :]
        dk_own[g, :, HEAD:] = dv[BLOCK - TOK :]
        each(BLOCK // TOK, lambda i: dk_send(g, b * (BLOCK // TOK) + i))

    def query_gradient(g):
        qgr[:, part(g, WIDE)] = turned(dot(kt[...], dscore[...]) * SCALE).astype(BF16)
        qgr_copy(g).start()

    def dk_copy(g, w, a, to):
        return remote(
            dk_out.at[g, part(w + SIDE * a, TOK), :], dk_in.at[g, w - 1, a],
            dk_s.at[g, w - 1, a], dk_r.at[g, w - 1, a], seq=to,
        )

    def dk_send(g, slot, wait=False):
        w, a = lax.rem(slot, SIDE), slot // SIDE

        @pl.when((w != 0) & (slot < BACK) & (me + slot >= BACK))
        def _():
            go(dk_copy(g, jnp.maximum(w, 1), a, y * SIDE + lax.rem(z + w, SIDE)), wait)

    def dc_copy(g, rows):
        return remote(
            dk_row.at[g, rows - 1], dk_col.at[g, rows - 1],
            dc_s.at[g, rows - 1], dc_r.at[g, rows - 1],
            seq=jnp.maximum(me - SIDE * rows, 0),
        )

    def dc_send(g, wait=False):
        for rows in (1, 2):
            @pl.when(y >= rows)
            def _():
                go(dc_copy(g, rows), wait)

    def row_sum(g):
        dk_sum[0] = dk_own[g]
        dk_sum[1] = dk_out[g, SIDE * TOK : (SIDE + 1) * TOK, :].astype(F32)
        dk_sum[2] = dk_out[g, :TOK, :].astype(F32)
        for w in range(1, SIDE):
            source = y * SIDE + lax.rem(z + SIDE - w, SIDE)
            nearer = jnp.where(z < w, 0, 1)
            for a in range(2):
                @pl.when(source + w + SIDE * a >= BACK)
                def _():
                    dk_copy(g, w, a, me).wait_recv()
                    at = nearer + 1 - a
                    dk_sum[at] = dk_sum[at] + dk_in[g, w - 1, a].astype(F32)

        dk_own[g] = dk_sum[0]
        dk_row[g, 0] = dk_sum[1].astype(BF16)
        dk_row[g, 1] = dk_sum[2].astype(BF16)
        dc_send(g)

    partner = row + 1 - 2 * lax.rem(row, 2)

    def ag_copy(g, message, slot, peer):
        block = dall.at[g, part(slot, TOK), :]
        return remote(block, block, ag_s.at[g, message], ag_r.at[g, slot], dp=peer)

    def along_x(i):
        return lax.rem(row + 2 + 2 * i, N_DP)

    def ag_send(g, wait=False):
        each(SIDE - 1, lambda i: go(ag_copy(g, i, row, along_x(i)), wait))
        go(ag_copy(g, SIDE - 1, row, partner), wait)

    def ag_relay(g, wait=False):
        def one(i):
            copy = ag_copy(g, SIDE + i, along_x(i), partner)
            if not wait:
                copy.wait_recv()
            go(copy, wait)

        each(SIDE - 1, one)

    def home(g):
        dk_sum[0] = dk_own[g]
        for rows in (1, 2):
            @pl.when(y + rows < SIDE)
            def _():
                dc_copy(g, rows).wait_recv()
                dk_sum[0] = dk_sum[0] + dk_col[g, rows - 1].astype(F32)

        half = dk_sum[0].astype(BF16)
        dall[g, part(row, TOK), :] = half
        ag_send(g)
        dkvt[part(g, PAIR), :] = half.T

    def rs_copy(g, i, slot, peer):
        return remote(
            w_out.at[g, part(peer, D_OWN), :], w_in.at[g, slot],
            rs_s.at[g, i], rs_r.at[g, slot], seq=peer,
        )

    def rs_send(g, wait=False):
        each(N_SEQ - 1, lambda i: go(rs_copy(g, i, me, other(me, i, N_SEQ)), wait))

    def product(g):
        ag_relay(g)
        each(SIDE, lambda i: ag_copy(g, 0, lax.rem(partner + 2 * i, N_DP), partner).wait_recv())

        w_out[g] = dot(hxt[...], dall[g]).astype(BF16)
        rs_send(g)

    def finish(g):
        def arrive(i, total):
            peer = other(me, i, N_SEQ)
            rs_copy(g, i, peer, peer).wait_recv()
            return total + w_in[g, peer].astype(F32)

        own = w_out[g, part(me, D_OWN), :].astype(F32)
        wgr[:, part(g, PAIR)] = lax.fori_loop(0, N_SEQ - 1, arrive, own) * FACTOR

    def hgr_copy(i):
        cols = part(i, HG)
        return pltpu.make_async_copy(hgr.at[:, cols], hgrad_hbm.at[:, cols], out_sem.at[2, i])

    def hidden_gradient(g, i):
        cols = part(i, HG)
        term = dot(wgt[g, cols, :], dkvt[part(g, PAIR), :])

        @pl.when(g == 0)
        def _():
            hgr_sum[cols, :] = term

        @pl.when((g > 0) & (g < GROUPS - 1))
        def _():
            hgr_sum[cols, :] += term

        @pl.when(g == GROUPS - 1)
        def _():
            hgr[:, cols] = (hgr_sum[cols, :] + term).T.astype(BF16)
            hgr_copy(i).start()

    def stage(g):
        kv_rest(g)
        forward(g)

        @pl.when(g == 0)
        def _():
            kv_second(3)

        @pl.when(g == 2)
        def _():
            hx_arrive()

        @pl.when(g >= 2)
        def _():
            row_sum(g - 2)

        each(KEYS // BLOCK, lambda b: backward(g, b))
        query_gradient(g)


    def hidden_part(g):
        each(D // HG, lambda i: hidden_gradient(g, i))

    each(GROUPS, stage)
    home(0)
    hidden_part(0)
    row_sum(2)
    home(1)
    hidden_part(1)
    product(0)
    row_sum(3)
    home(2)
    product(1)
    hidden_part(2)
    home(3)
    product(2)
    hidden_part(3)
    product(3)
    finish(0)
    finish(1)
    finish(2)
    finish(3)
    wgr_copy = pltpu.make_async_copy(wgr, wgrad_hbm, in_sem.at[4])
    wgr_copy.start()

    def drain(g):
        kv_first(g, True)
        kv_second(g, True)
        each(BACK, lambda i: dk_send(g, i, True))
        dc_send(g, True)
        ag_send(g, True)
        ag_relay(g, True)
        rs_send(g, True)
        att_copy(g).wait()
        qgr_copy(g).wait()

    each(GROUPS, drain)
    each(N_DP - 1, lambda i: hx_copy(i, row, other(row, i, N_DP)).wait_send())
    each(D // HG, lambda i: hgr_copy(i).wait())
    wgr_copy.wait()


def local(hidden, queries, kv_weight, value_projection_bias, cotangent, lengths):
    any_spec = pl.BlockSpec(memory_space=pl.ANY)
    vmem = pltpu.VMEM
    dma = pltpu.SemaphoreType.DMA
    width = GROUPS * GROUP_HEADS * HEAD
    return pl.pallas_call(
        kernel,
        out_shape=(
            jax.ShapeDtypeStruct((TOK, width), BF16),
            jax.ShapeDtypeStruct((TOK, width), BF16),
            jax.ShapeDtypeStruct((TOK, D), BF16),
            jax.ShapeDtypeStruct((D_OWN, GROUPS * PAIR), F32),
        ),
        in_specs=[
            any_spec,
            any_spec,
            any_spec,
            pl.BlockSpec(memory_space=pltpu.VMEM),
            any_spec,
            pl.BlockSpec(memory_space=pltpu.SMEM),
        ],
        out_specs=(any_spec,) * 4,
        scratch_shapes=[
            vmem((TOK, D), BF16),
            vmem((TOK, width), BF16),
            vmem((TOK, width), BF16),
            vmem((GROUPS, D, PAIR), BF16),
            vmem((GROUPS, KEYS, PAIR), BF16),
            vmem((KEYS, TOK), F32),
            vmem((HEAD, KEYS), BF16),
            vmem((HEAD, KEYS), BF16),
            vmem((GROUP_HEADS * HEAD, HEAD), BF16),
            vmem((GROUP_HEADS * HEAD, HEAD), BF16),
            vmem((HEAD, GROUP_HEADS * HEAD), BF16),
            vmem((1, GROUP_HEADS * HEAD), F32),
            vmem((KEYS, GROUP_HEADS * HEAD), BF16),
            vmem((KEYS, GROUP_HEADS * HEAD), BF16),
            vmem((TOK, width), BF16),
            vmem((TOK, width), BF16),
            vmem((TOK, D), BF16),
            vmem((D, TOK), F32),
            vmem((D_OWN, GROUPS * PAIR), F32),
            vmem((GROUPS, KEYS, PAIR), BF16),
            vmem((GROUPS, SIDE - 1, 2, TOK, PAIR), BF16),
            vmem((3, TOK, PAIR), F32),
            vmem((GROUPS, 2, TOK, PAIR), BF16),
            vmem((GROUPS, 2, TOK, PAIR), BF16),
            vmem((GROUPS, TOK, PAIR), F32),
            vmem((GROUPS * PAIR, TOK), BF16),
            vmem((N_DP * TOK, D_PART), BF16),
            vmem((D_PART, N_DP * TOK), BF16),
            vmem((GROUPS, N_DP * TOK, PAIR), BF16),
            vmem((GROUPS, D_PART, PAIR), BF16),
            vmem((GROUPS, N_SEQ, D_OWN, PAIR), BF16),
            dma((5,)),
            dma((GROUPS,)),
            dma((GROUPS, 11)),
            dma((GROUPS, BACK)),
            dma((GROUPS, SIDE - 1, 2)),
            dma((GROUPS, SIDE - 1, 2)),
            dma((GROUPS, 2)),
            dma((GROUPS, 2)),
            dma((N_DP,)),
            dma((N_DP,)),
            dma((GROUPS, N_DP)),
            dma((GROUPS, N_DP)),
            dma((GROUPS, N_SEQ)),
            dma((GROUPS, N_SEQ)),
            dma((3, 16)),
        ],
        compiler_params=pltpu.CompilerParams(
            collective_id=0, has_side_effects=True, vmem_limit_bytes=60 * 1024 * 1024
        ),
        cost_estimate=pl.CostEstimate(
            flops=14_000_000_000, bytes_accessed=26_000_000, transcendentals=5_000_000
        ),
    )(
        hidden,
        queries,
        kv_weight,
        value_projection_bias.reshape(GROUPS, 1, HEAD),
        cotangent,
        lengths,
    )


def solution(mesh):
    both = P(("dp", "seq"), None)
    return jax.shard_map(
        local,
        mesh=mesh,
        in_specs=(both, both, P(), P(), both, P("dp", None)),
        out_specs=(both,) * 4,
        check_vma=False,
    )
```

time: 119 us -> 102 us (0.86)
  Pallas kernels: 113 us -> 95.5 us
    pallas_call x1, Pallas kernels: 113 us -> 95.5 us  [local(): pl.pallas_call(kernel, out_shape=(jax.ShapeDtypeStruct((TOK, width), BF16...]
where the time goes in v3:
time: 102 us
  Pallas kernels  95.5 us (94%)
  local copies, waits for them, and re-layouts  5.44 us (5%)
    pallas_call x1, Pallas kernels, local(): pl.pallas_call(kernel, out_shape=(jax.ShapeDtypeStruct((TOK, width), BF16...  95.5 us
    unnamed x10, local copies, waits for them, and re-layouts  5.44 us

profile of v3, /device:TPU:1, one launch (start us, length us, event | category | flops | bytes accessed | tf_op | source)
XLA Modules:
  0.0 101.6 jit_solution(8875927811821989700)
XLA Ops:
  0.6 95.5 %shard_map.93 = (bf16[128,4096]{1,0:T(8,128)(2,1)}, bf16[128,4096]{1,0:T(8,128)(2,1)}, bf16[128,8192]{1,0:T(8,128)(2,1)}, f32[64,1024]{1,0:T(8,128)}) custom-call(bf16[128,8192]{1,0:T(8,128)(2,1)} %hidden_hbm.1, bf16[128,4096]{1,0:T(8,128)(2,1)} %queries_hbm.1, bf16[8192,1024]{1,0:T(8,128)(2,1)} %weight_hbm.1, f32[4,1,128]{2,1,0:T(1,128)} %bitcast.1, ...), custom_call_target="tpu_custom_call" | custom-call | flops 14000000000 | bytes 26000000 | tf_op jit(solution)/shard_map/pallas_call | solution.py:477
  96.2 0.0 copy-start.1
  96.2 0.0 copy-start
  96.2 2.4 %copy.14 = bf16[128,4096]{1,0:T(8,128)(2,1)} copy(bf16[128,4096]{1,0:T(8,128)(2,1)} %get-tuple-element.8) | data formatting | bytes 2097152
  98.6 0.0 copy-done.1
  98.6 1.0 copy.15
  99.6 0.0 copy-done
  99.6 0.0 copy-start.2
  99.6 1.3 %copy.16 = bf16[128,8192]{1,0:T(8,128)(2,1)} copy(bf16[128,8192]{1,0:T(8,128)(2,1)S(1)} %copy-done) | data formatting | bytes 4194304
  100.9 0.0 copy-done.2
  100.9 0.7 copy.17
Async XLA Ops:
  96.2 2.5 %copy-start.1 = (bf16[128,4096]{1,0:T(8,128)(2,1)S(1)}, bf16[128,4096]{1,0:T(8,128)(2,1)}, u32[]{:S(2)}) copy-start(bf16[128,4096]{1,0:T(8,128)(2,1)} %get-tuple-element.9) | copy-start | bytes 3145732
  96.2 3.4 %copy-start = (bf16[128,8192]{1,0:T(8,128)(2,1)S(1)}, bf16[128,8192]{1,0:T(8,128)(2,1)}, u32[]{:S(2)}) copy-start(bf16[128,8192]{1,0:T(8,128)(2,1)} %get-tuple-element.10) | copy-start | bytes 6291460
  99.6 1.3 %copy-start.2 = (f32[64,1024]{1,0:T(8,128)S(1)}, f32[64,1024]{1,0:T(8,128)}, u32[]{:S(2)}) copy-start(f32[64,1024]{1,0:T(8,128)} %get-tuple-element.11) | copy-start | bytes 786436

commit v4 on v3

--- a/solution.py
+++ b/solution.py
@@ -23,7 +23,7 @@
 D_OWN = D_PART // N_SEQ
 SIDE = 4
 BLOCK = 3 * TOK
-HG = 2048
+HG = 4096
 SCALE = 1.0 / math.sqrt(HEAD)
 LOG2E = 1.4426950408889634
 FACTOR = 1.0 / math.sqrt(TOK * N_DP * N_SEQ)
@@ -110,6 +110,23 @@
     each(jnp.maximum(BACK - me, 0), clear)
 
     in_hid.wait()
+
+    def project(g):
+        weight_copy(g).wait()
+
+        @pl.when(g + 2 < GROUPS)
+        def _():
+            weight_copy(g + 2).start()
+
+        def step(i, total):
+            cols = part(i, 4096)
+            return total + dot(hid[:, cols], wgt[g, cols, :])
+
+        total = lax.fori_loop(0, D // 4096, step, jnp.zeros((TOK, PAIR), F32))
+        kv[g, BACK * TOK :, :HEAD] = total[:, :HEAD].astype(BF16)
+        kv[g, BACK * TOK :, HEAD:] = (total[:, HEAD:] + bias_ref[g]).astype(BF16)
+
+    project(0)
     pl.semaphore_wait(barrier, N_SEQ - 1 + N_DP - 1)
 
     def kv_send(g, message, src, dst, peer):
@@ -130,8 +147,12 @@
                 to = jnp.minimum(me + SIDE * rows, N_SEQ - 1)
                 go(kv_send(g, rows - 1, BACK, BACK - SIDE * rows, to), wait)
 
+    def sent(g, i):
+        return (i != 1) | (g == 0)
+
+    def kv_row(g, wait=False):
         def own(i):
-            @pl.when(other(z, i, SIDE) > z)
+            @pl.when((other(z, i, SIDE) > z) & sent(g, i))
             def _():
                 along_z(g, i, 2, BACK, wait)
 
@@ -141,11 +162,22 @@
         kv_send(g, 0, BACK, s, me).wait_recv()
 
     def kv_second(g, wait=False):
+        if not wait:
+            @pl.when(g > 0)
+            def _():
+                kv_row(g)
+
         @pl.when(y >= 1)
         def _():
             if not wait:
                 kv_arrive(g, SIDE)
-            each(SIDE - 1, lambda i: along_z(g, i, 5, SIDE, wait))
+
+            def row_before(i):
+                @pl.when(sent(g, i))
+                def _():
+                    along_z(g, i, 5, SIDE, wait)
+
+            each(SIDE - 1, row_before)
 
         @pl.when(y >= 2)
         def _():
@@ -153,34 +185,35 @@
                 kv_arrive(g, 0)
 
             def two_before(i):
-                @pl.when(other(z, i, SIDE) < z)
+                @pl.when((other(z, i, SIDE) < z) & sent(g, i))
                 def _():
                     along_z(g, i, 8, 0, wait)
 
             each(SIDE - 1, two_before)
 
+    up_from = jnp.where(z == SIDE - 1, 3, 7)
+    down_from = jnp.where(z == 0, 5, 1)
+
+    def kv_third(g, wait=False):
+        for message, src, dst, to in (
+            (11, up_from, 6, y * SIDE + lax.rem(z + 1, SIDE)),
+            (12, down_from, 2, y * SIDE + lax.rem(z + SIDE - 1, SIDE)),
+        ):
+            @pl.when(me + src >= BACK)
+            def _():
+                if not wait:
+                    kv_arrive(g, src)
+                go(kv_send(g, message, src, dst, to), wait)
+
     def kv_rest(g):
         def arrive(s):
-            @pl.when((lax.rem(s, SIDE) != 0) & (me + s >= BACK))
+            passed = (g > 0) & ((s == up_from) | (s == down_from))
+
+            @pl.when((lax.rem(s, SIDE) != 0) & (me + s >= BACK) & jnp.logical_not(passed))
             def _():
                 kv_arrive(g, s)
 
         each(BACK, arrive)
-
-    def project(g):
-        weight_copy(g).wait()
-
-        @pl.when(g + 2 < GROUPS)
-        def _():
-            weight_copy(g + 2).start()
-
-        def step(i, total):
-            cols = part(i, 2048)
-            return total + dot(hid[:, cols], wgt[g, cols, :])
-
-        total = lax.fori_loop(0, D // 2048, step, jnp.zeros((TOK, PAIR), F32))
-        kv[g, BACK * TOK :, :HEAD] = total[:, :HEAD].astype(BF16)
-        kv[g, BACK * TOK :, HEAD:] = (total[:, HEAD:] + bias_ref[g]).astype(BF16)
 
     def hx_copy(i, slot, peer):
         return remote(
@@ -192,9 +225,15 @@
         hid.at[:, part(row, D_PART)], hx.at[part(row, TOK), :], in_sem.at[3]
     )
     def prepare(t):
-        project(t)
+        @pl.when(t > 0)
+        def _():
+            project(t)
 
         kv_first(t)
+
+        @pl.when(t == 0)
+        def _():
+            kv_row(t)
 
         @pl.when(t == 0)
         def _():
@@ -220,10 +259,7 @@
         each(N_DP - 1, arrive)
         hx_own.wait()
 
-        def turn(i):
-            hxt[:, part(i, TOK)] = hx[part(i, TOK), :].T
-
-        each(N_DP, turn)
+        hxt[...] = hx[...].T
 
     def att_copy(g):
         cols = part(g, 1024)
@@ -409,11 +445,20 @@
 
     def stage(g):
         kv_rest(g)
+
+        @pl.when(g == 0)
+        def _():
+            kv_third(1)
+
         forward(g)
 
         @pl.when(g == 0)
         def _():
             kv_second(3)
+
+        @pl.when(g < 2)
+        def _():
+            kv_third(g + 2)
 
         @pl.when(g == 2)
         def _():
@@ -448,25 +493,55 @@
     finish(0)
     finish(1)
     finish(2)
-    finish(3)
-    wgr_copy = pltpu.make_async_copy(wgr, wgrad_hbm, in_sem.at[4])
-    wgr_copy.start()
 
     def drain(g):
         kv_first(g, True)
+        kv_row(g, True)
         kv_second(g, True)
+
+        @pl.when(g > 0)
+        def _():
+            kv_third(g, True)
+
         each(BACK, lambda i: dk_send(g, i, True))
         dc_send(g, True)
         ag_send(g, True)
         ag_relay(g, True)
-        rs_send(g, True)
         att_copy(g).wait()
         qgr_copy(g).wait()
 
     each(GROUPS, drain)
     each(N_DP - 1, lambda i: hx_copy(i, row, other(row, i, N_DP)).wait_send())
     each(D // HG, lambda i: hgr_copy(i).wait())
+    finish(3)
+    wgr_copy = pltpu.make_async_copy(wgr, wgrad_hbm, in_sem.at[4])
+    wgr_copy.start()
+
+    def rs_end(g):
+        rs_send(g, True)
+
+    each(GROUPS, rs_end)
     wgr_copy.wait()
+
+
+def settle(a_in, b_in, c_in, d_in, a_out, b_out, c_out, d_out, a, b, c, d, sems):
+    parts = []
+    for src, mid, dst in ((a_in, a, a_out), (b_in, b, b_out), (c_in, c, c_out), (d_in, d, d_out)):
+        half = src.shape[0] // 2
+        for h in range(2):
+            rows = pl.ds(h * half, half)
+            k = len(parts)
+            parts.append((
+                pltpu.make_async_copy(src.at[rows], mid.at[rows], sems.at[0, k]),
+                pltpu.make_async_copy(mid.at[rows], dst.at[rows], sems.at[1, k]),
+            ))
+    for fetch, _ in parts:
+        fetch.start()
+    for fetch, store in parts:
+        fetch.wait()
+        store.start()
+    for _, store in parts:
+        store.wait()
 
 
 def local(hidden, queries, kv_weight, value_projection_bias, cotangent, lengths):
@@ -474,7 +549,7 @@
     vmem = pltpu.VMEM
     dma = pltpu.SemaphoreType.DMA
     width = GROUPS * GROUP_HEADS * HEAD
-    return pl.pallas_call(
+    results = pl.pallas_call(
         kernel,
         out_shape=(
             jax.ShapeDtypeStruct((TOK, width), BF16),
@@ -525,7 +600,7 @@
             vmem((GROUPS, N_SEQ, D_OWN, PAIR), BF16),
             dma((5,)),
             dma((GROUPS,)),
-            dma((GROUPS, 11)),
+            dma((GROUPS, 13)),
             dma((GROUPS, BACK)),
             dma((GROUPS, SIDE - 1, 2)),
             dma((GROUPS, SIDE - 1, 2)),
@@ -553,6 +628,13 @@
         cotangent,
         lengths,
     )
+    return pl.pallas_call(
+        settle,
+        out_shape=tuple(jax.ShapeDtypeStruct(r.shape, r.dtype) for r in results),
+        in_specs=[any_spec] * 4,
+        out_specs=(any_spec,) * 4,
+        scratch_shapes=[vmem(r.shape, r.dtype) for r in results] + [dma((2, 8))],
+    )(*results)
 
 
 def solution(mesh):

time: 102 us -> 93.1 us (0.913)
  local copies, waits for them, and re-layouts: 5.44 us -> 0 us
  Pallas kernels: 95.5 us -> 92.3 us
    pallas_call x1, Pallas kernels: 95.5 us -> 88.5 us  [local(): pl.pallas_call(kernel, out_shape=(jax.ShapeDtypeStruct((TOK, width), BF16...]
    unnamed x10 -> x0, local copies, waits for them, and re-layouts: 5.44 us -> none
    pallas_call x0 -> x1, Pallas kernels: none -> 3.86 us  [local(): pl.pallas_call(settle, out_shape=tuple((jax.ShapeDtypeStruct(r.shape, r.d...]
where the time goes in v4:
time: 93.1 us; the launch traced here: 93 us
  Pallas kernels  92.3 us (99%)
    pallas_call x1, Pallas kernels, local(): pl.pallas_call(kernel, out_shape=(jax.ShapeDtypeStruct((TOK, width), BF16...  88.5 us
    pallas_call x1, Pallas kernels, local(): pl.pallas_call(settle, out_shape=tuple((jax.ShapeDtypeStruct(r.shape, r.d...  3.86 us

profile of v4, /device:TPU:1, one launch (start us, length us, event | category | flops | bytes accessed | tf_op | source)
XLA Modules:
  0.0 93.0 jit_solution(10118630082320566675)
XLA Ops:
  0.6 88.5 %shard_map.93 = (bf16[128,4096]{1,0:T(8,128)(2,1)}, bf16[128,4096]{1,0:T(8,128)(2,1)}, bf16[128,8192]{1,0:T(8,128)(2,1)}, f32[64,1024]{1,0:T(8,128)}) custom-call(bf16[128,8192]{1,0:T(8,128)(2,1)} %hidden_hbm.1, bf16[128,4096]{1,0:T(8,128)(2,1)} %queries_hbm.1, bf16[8192,1024]{1,0:T(8,128)(2,1)} %weight_hbm.1, f32[4,1,128]{2,1,0:T(1,128)} %bitcast.1, ...), custom_call_target="tpu_custom_call" | custom-call | flops 14000000000 | bytes 26000000 | tf_op jit(solution)/shard_map/pallas_call | solution.py:552
  89.1 3.9 %shard_map.94 = (bf16[128,4096]{1,0:T(8,128)(2,1)}, bf16[128,4096]{1,0:T(8,128)(2,1)}, bf16[128,8192]{1,0:T(8,128)(2,1)}, f32[64,1024]{1,0:T(8,128)}) custom-call(bf16[128,4096]{1,0:T(8,128)(2,1)} %get-tuple-element.8.a_in, bf16[128,4096]{1,0:T(8,128)(2,1)} %get-tuple-element.9.b_in, bf16[128,8192]{1,0:T(8,128)(2,1)} %get-tuple-element.10.c_in, ...), custom_call_target="tpu_custom_call" | custom-call | tf_op jit(solution)/shard_map/pallas_call | solution.py:631

commit v5 on v4

--- a/solution.py
+++ b/solution.py
@@ -468,6 +468,10 @@
         def _():
             row_sum(g - 2)
 
+        @pl.when(g == 3)
+        def _():
+            home(0)
+
         each(KEYS // BLOCK, lambda b: backward(g, b))
         query_gradient(g)
 
@@ -476,13 +480,12 @@
         each(D // HG, lambda i: hidden_gradient(g, i))
 
     each(GROUPS, stage)
-    home(0)
     hidden_part(0)
     row_sum(2)
     home(1)
     hidden_part(1)
+    row_sum(3)
     product(0)
-    row_sum(3)
     home(2)
     product(1)
     hidden_part(2)

time: 93.1 us -> 90.9 us (0.976)
  Pallas kernels: 92.3 us -> 90.1 us
    pallas_call x1, Pallas kernels: 88.5 us -> 86.2 us  [local(): pl.pallas_call(kernel, out_shape=(jax.ShapeDtypeStruct((TOK, width), BF16...]
where the time goes in v5:
time: 90.9 us; the launch traced here: 90.7 us
  Pallas kernels  90.1 us (99%)
    pallas_call x1, Pallas kernels, local(): pl.pallas_call(kernel, out_shape=(jax.ShapeDtypeStruct((TOK, width), BF16...  86.2 us
    pallas_call x1, Pallas kernels, local(): pl.pallas_call(settle, out_shape=tuple((jax.ShapeDtypeStruct(r.shape, r.d...  3.86 us

profile of v5, /device:TPU:1, one launch (start us, length us, event | category | flops | bytes accessed | tf_op | source)
XLA Modules:
  0.0 90.7 jit_solution(7609987321549267982)
XLA Ops:
  0.6 86.2 %shard_map.93 = (bf16[128,4096]{1,0:T(8,128)(2,1)}, bf16[128,4096]{1,0:T(8,128)(2,1)}, bf16[128,8192]{1,0:T(8,128)(2,1)}, f32[64,1024]{1,0:T(8,128)}) custom-call(bf16[128,8192]{1,0:T(8,128)(2,1)} %hidden_hbm.1, bf16[128,4096]{1,0:T(8,128)(2,1)} %queries_hbm.1, bf16[8192,1024]{1,0:T(8,128)(2,1)} %weight_hbm.1, f32[4,1,128]{2,1,0:T(1,128)} %bitcast.1, ...), custom_call_target="tpu_custom_call" | custom-call | flops 14000000000 | bytes 26000000 | tf_op jit(solution)/shard_map/pallas_call | solution.py:555
  86.9 3.9 %shard_map.94 = (bf16[128,4096]{1,0:T(8,128)(2,1)}, bf16[128,4096]{1,0:T(8,128)(2,1)}, bf16[128,8192]{1,0:T(8,128)(2,1)}, f32[64,1024]{1,0:T(8,128)}) custom-call(bf16[128,4096]{1,0:T(8,128)(2,1)} %get-tuple-element.8.a_in, bf16[128,4096]{1,0:T(8,128)(2,1)} %get-tuple-element.9.b_in, bf16[128,8192]{1,0:T(8,128)(2,1)} %get-tuple-element.10.c_in, ...), custom_call_target="tpu_custom_call" | custom-call | tf_op jit(solution)/shard_map/pallas_call | solution.py:634
